TPU v7x, 128 devices: a whole 4x4x4 slice. The times are simulated.
128 devices in a mesh: section: 2 (over core), dp: 8 (over x, y_lo), seq: 8 (over z, y_hi).
Axes of the slice: x: 4, y: 4 (y_hi: 2, y_lo: 2; y = y_hi * 2 + y_lo), z: 4, core: 2. Of those that a mesh axis runs over, the one named last changes fastest.
Arguments:
- inputs: bfloat16 [2, 8, 1024, 1024], P(None, 'dp', 'seq'), may hold values from -6 to 6
- cotangent: bfloat16 [2, 8, 1024, 1024], P(None, 'dp', 'seq'), may hold values from -6 to 6
- conv_in: bfloat16 [1024, 3072], P(('section', 'dp', 'seq')), may hold values from -0.1875 to 0.1875
- conv_kernel: bfloat16 [3, 1024], P(None, ('section', 'dp', 'seq')), may hold values from -3.5 to 3.5
- qkv_weight: bfloat16 [1024, 2048], P(('section', 'dp', 'seq')), may hold values from -0.1875 to 0.1875
- qk_gain: bfloat16 [2, 64], replicated, may hold values from 0.5 to 1.5
- mix_gain: bfloat16 [2, 1024], P('section'), may hold values from 0.5 to 1.5
- ffn_gain: bfloat16 [2, 1024], P('section'), may hold values from 0.5 to 1.5
- mix_out: bfloat16 [2, 1024, 1024], P('section', ('dp', 'seq')), may hold values from -0.375 to 0.375
- w_gate: bfloat16 [2, 1024, 4608], P('section', ('dp', 'seq')), may hold values from -0.1875 to 0.1875
- w_up: bfloat16 [2, 1024, 4608], P('section', ('dp', 'seq')), may hold values from -0.1875 to 0.1875
- w_down: bfloat16 [2, 4608, 1024], P('section', None, ('dp', 'seq')), may hold values from -0.09375 to 0.09375
Outputs:
- outputs: bfloat16 [2, 8, 1024, 1024], P(None, 'dp', 'seq', 'section')
- input_grad: bfloat16 [2, 8, 1024, 1024], P(None, 'dp', 'seq', 'section')
- conv_in_grad: float32 [1024, 3072], P(('section', 'dp', 'seq'))
- conv_kernel_grad: float32 [3, 1024], P(None, ('section', 'dp', 'seq'))
- qkv_grad: float32 [1024, 2048], P(('section', 'dp', 'seq'))
- qk_gain_grad: float32 [2, 64], replicated
- mix_gain_grad: float32 [2, 1024], P('section')
- ffn_gain_grad: float32 [2, 1024], P('section')
- mix_out_grad: float32 [2, 1024, 1024], P('section', ('dp', 'seq'))
- gate_grad: float32 [2, 1024, 4608], P('section', ('dp', 'seq'))
- up_grad: float32 [2, 1024, 4608], P('section', ('dp', 'seq'))
- down_grad: float32 [2, 4608, 1024], P('section', None, ('dp', 'seq'))
All inputs are finite; a program needn't handle non-finite values.
Results may differ from a plain program's by a relative error of at most 0.018.
Values may be sent and summed in bfloat16 or wider, within the bound.
A program may use at most 384 MiB of HBM per device.

v0:
```python
import functools

import jax
import jax.numpy as jnp
from jax import lax
from jax.experimental import pallas as pl
from jax.experimental.pallas import tpu as pltpu
from jax.sharding import PartitionSpec as P

EPSILON = 1e-05
S, DP, SQ = "section", "dp", "seq"
MESH = pl.DeviceIdType.MESH
ANY = pl.BlockSpec(memory_space=pl.ANY)
BF, F32 = jnp.bfloat16, jnp.float32
ORDERS = ((0, 1, 2), (1, 2, 0), (2, 0, 1))
MIB = 2**20


def chip():
    dp, sq = lax.axis_index(DP), lax.axis_index(SQ)
    return (dp // 2, 2 * (sq % 2) + dp % 2, sq // 2)


def device_at(place):
    x, y, z = place
    return {DP: x * 2 + y % 2, SQ: z * 2 + y // 2}


def moved(place, axis, by):
    return tuple((v + by) % 4 if i == axis else v for i, v in enumerate(place))


def spot(place, kept=(0, 1, 2)):
    x, y, z = place

    def one(axis, value, take):
        if axis not in kept:
            return 0
        return slice(None) if value is None else take(value)

    return (
        one(0, x, lambda v: v),
        one(1, y, lambda v: v % 2),
        one(2, z, lambda v: v),
        one(1, y, lambda v: v // 2),
    )


def halves(width):
    first = (width // 256) * 128
    return (pl.ds(0, first), pl.ds(first, width - first))


def greet(devices):
    barrier = pltpu.get_barrier_semaphore()
    for device in devices:
        pl.semaphore_signal(barrier, inc=1, device_id=device, device_id_type=MESH)
    pl.semaphore_wait(barrier, len(devices))


def neighbours():
    here = chip()
    return [device_at(moved(here, axis, by)) for axis in range(3) for by in (1, -1)]


class Gather:
    def __init__(self, bufs, send, recv):
        self.bufs, self.send, self.recv = bufs, send, recv
        self.here = chip()

    def copy(self, colour, phase, kind):
        order = ORDERS[colour]
        axis, done = order[phase], order[:phase]
        buf = self.bufs[colour]
        half = halves(buf.shape[-1])
        step, part, to = ((0, 0, 1), (0, 1, 1), (0, 1, -1), (0, 0, -1), (-1, 0, 1), (1, 1, -1))[kind]
        source = moved(self.here, axis, step)
        block = tuple(None if i in done else v for i, v in enumerate(source))
        ref = buf.at[spot(block) + (slice(None), half[part])]
        slot = (colour * 3 + phase) * 6 + kind
        return pltpu.make_async_remote_copy(
            src_ref=ref,
            dst_ref=ref,
            send_sem=self.send.at[slot],
            recv_sem=self.recv.at[slot],
            device_id=device_at(moved(self.here, axis, to)),
            device_id_type=MESH,
        )

    def start(self, phase):
        for pair in ((0, 2), (1, 3)):
            for kind in pair:
                for colour in range(3):
                    self.copy(colour, phase, kind).start()

    def forward(self, phase):
        for got, then in ((0, 4), (2, 5)):
            for colour in range(3):
                self.copy(colour, phase, got).wait_recv()
                self.copy(colour, phase, then).start()

    def finish(self, phase):
        for kind in (1, 3, 4, 5):
            for colour in range(3):
                self.copy(colour, phase, kind).wait_recv()

    def settle(self):
        for phase in range(3):
            for kind in range(6):
                for colour in range(3):
                    self.copy(colour, phase, kind).wait_send()


def gather_kernel(*refs):
    shards, bufs, (own, send, recv) = refs[:3], refs[3:6], refs[6:]
    here = chip()
    greet(neighbours())
    local = [
        pltpu.make_async_copy(shards[c], bufs[c].at[spot(here)], own.at[c]) for c in range(3)
    ]
    for copy in local:
        copy.start()
    for copy in local:
        copy.wait()
    ring = Gather(bufs, send, recv)
    for phase in range(3):
        ring.start(phase)
        ring.forward(phase)
        ring.finish(phase)
    ring.settle()


def gathered(shards, cid):
    return pl.pallas_call(
        gather_kernel,
        name="gather",
        out_shape=[jax.ShapeDtypeStruct((4, 2, 4, 2) + s.shape, s.dtype) for s in shards],
        in_specs=[ANY] * 3,
        out_specs=[ANY] * 3,
        scratch_shapes=[
            pltpu.SemaphoreType.DMA((3,)),
            pltpu.SemaphoreType.DMA((54,)),
            pltpu.SemaphoreType.DMA((54,)),
        ],
        compiler_params=pltpu.CompilerParams(collective_id=cid, has_side_effects=True),
    )(*shards)


def lead(kept):
    return (4 if 0 in kept else 1, 2 if 1 in kept else 1, 4 if 2 in kept else 1, 2 if 1 in kept else 1)


def one_block(place, axis):
    x, y, z = place
    every = slice(None)
    return (
        pl.ds(x, 1) if axis == 0 else every,
        pl.ds(y % 2, 1) if axis == 1 else every,
        pl.ds(z, 1) if axis == 2 else every,
        pl.ds(y // 2, 1) if axis == 1 else every,
        every,
    )


def scatter_scratch(widths):
    shapes = []
    for colour, width in enumerate(widths):
        for phase in range(3):
            rows = lead(ORDERS[colour][phase + 1 :]) + (16,)
            pair = [rows + (h.size,) for h in halves(width)]
            shapes += [rows + (width,)] + pair + pair + [rows + (width,)] * 2
    return [pltpu.VMEM(s, BF) for s in shapes]


class Scatter:
    def __init__(self, parts, bufs, results, send, recv, load):
        self.parts, self.results = parts, results
        self.bufs = [[bufs[(c * 3 + p) * 7 :][:7] for p in range(3)] for c in range(3)]
        self.send, self.recv, self.load = send, recv, load
        self.here = chip()

    def source(self, colour, phase, by, half=None):
        axis = ORDERS[colour][phase]
        ref = self.parts[colour] if phase == 0 else self.bufs[colour][phase - 1][0]
        half = slice(None) if half is None else half
        return ref.at[one_block(moved(self.here, axis, by), axis) + (half,)]

    def loads(self, colour, phase):
        half = halves(self.parts[colour].shape[-1])
        own, ahead0, ahead1 = self.bufs[colour][phase][:3]
        pairs = (
            (self.source(colour, phase, 1, half[0]), ahead0),
            (self.source(colour, phase, -1, half[1]), ahead1),
            (self.source(colour, phase, 0), own),
        )
        return [
            functools.partial(pltpu.make_async_copy, a, b, self.load.at[(colour * 3 + phase) * 3 + i])
            for i, (a, b) in enumerate(pairs)
        ]

    def copy(self, colour, phase, kind):
        half = halves(self.parts[colour].shape[-1])
        own, ahead0, ahead1, first0, first1, last0, last1 = self.bufs[colour][phase]
        side = kind % 2
        to = (1, -1)[side]
        last = (last0, last1)[side]
        if kind < 2:
            src, dst = self.source(colour, phase, 2, half[side]), (first0, first1)[side]
        elif kind < 4:
            src, dst = self.source(colour, phase, to, half[1 - side]), last.at[..., half[1 - side]]
        else:
            src, dst = (ahead0, ahead1)[side], last.at[..., half[side]]
        slot = (colour * 3 + phase) * 6 + kind
        return pltpu.make_async_remote_copy(
            src_ref=src,
            dst_ref=dst,
            send_sem=self.send.at[slot],
            recv_sem=self.recv.at[slot],
            device_id=device_at(moved(self.here, ORDERS[colour][phase], to)),
            device_id_type=MESH,
        )

    def start(self, phase):
        for kind in range(4):
            for colour in range(3):
                self.copy(colour, phase, kind).start()
        for colour in range(3):
            for load in self.loads(colour, phase):
                load().start()

    def forward(self, phase):
        for side in range(2):
            for colour in range(3):
                self.loads(colour, phase)[side]().wait()
                self.copy(colour, phase, side).wait_recv()
                bufs = self.bufs[colour][phase]
                added(bufs[1 + side], (bufs[3 + side],), bufs[1 + side])
                self.copy(colour, phase, 4 + side).start()

    def finish(self, phase):
        for colour in range(3):
            self.loads(colour, phase)[2]().wait()
            for kind in range(2, 6):
                self.copy(colour, phase, kind).wait_recv()
            bufs = self.bufs[colour][phase]
            if phase < 2:
                added(bufs[0], (bufs[5], bufs[6]), bufs[0])
            else:
                added(bufs[0], (bufs[5], bufs[6]), self.results[colour])

    def settle(self):
        for phase in range(3):
            for kind in range(6):
                for colour in range(3):
                    self.copy(colour, phase, kind).wait_send()


def added(base, others, out):
    sizes = base.shape[:4]
    _, b, c, d = sizes

    def step(i, carry):
        at = (i // (b * c * d), (i // (c * d)) % b, (i // d) % c, i % d)
        total = base[at].astype(F32)
        for other in others:
            total = total + other[at].astype(F32)
        if len(out.shape) == 2:
            out[...] = total.astype(out.dtype)
        else:
            out[at] = total.astype(out.dtype)
        return carry

    lax.fori_loop(0, sizes[0] * b * c * d, step, 0)


class Small:
    def __init__(self, value, sums, other, slots, send, recv):
        self.value, self.sums, self.other, self.slots = value, sums, other, slots
        self.send, self.recv = send, recv
        self.here = chip()

    def sibling(self):
        return pltpu.make_async_remote_copy(
            src_ref=self.value.at[pl.ds(16, 8)],
            dst_ref=self.other,
            send_sem=self.send.at[9],
            recv_sem=self.recv.at[9],
            device_id={S: 1 - lax.axis_index(S)},
            device_id_type=MESH,
        )

    def copy(self, phase, by):
        slot = phase * 3 + by - 1
        return pltpu.make_async_remote_copy(
            src_ref=self.sums.at[phase],
            dst_ref=self.slots.at[slot],
            send_sem=self.send.at[slot],
            recv_sem=self.recv.at[slot],
            device_id=device_at(moved(self.here, phase, by)),
            device_id_type=MESH,
        )

    def start(self, phase):
        if phase == 0:
            self.sibling().start()
            self.sibling().wait_recv()
            self.sums[0] = self.value[...]
            self.sums[0, 16:24] = self.value[16:24] + self.other[...]
        for by in (1, 2, 3):
            self.copy(phase, by).start()

    def finish(self, phase):
        for by in (1, 2, 3):
            self.copy(phase, by).wait_recv()
        one, two, three = [self.slots[phase * 3 + i] for i in range(3)]
        self.sums[phase + 1] = (self.sums[phase] + two) + (one + three)

    def settle(self):
        self.sibling().wait_send()
        for phase in range(3):
            for by in (1, 2, 3):
                self.copy(phase, by).wait_send()


def line_mates():
    here = chip()
    return [device_at(moved(here, axis, by)) for axis in range(3) for by in (1, 2, 3)]


def scatter_kernel(with_small, *refs):
    refs = list(refs)
    parts = [refs.pop(0) for _ in range(3)]
    value = refs.pop(0) if with_small else None
    results = [refs.pop(0) for _ in range(3)]
    out = refs.pop(0) if with_small else None
    bufs, refs = refs[:63], refs[63:]
    send, recv, load = refs[:3]
    ring = Scatter(parts, bufs, results, send, recv, load)
    if with_small:
        sums, other, slots, ssend, srecv = refs[3:]
        small = Small(value, sums, other, slots, ssend, srecv)
        greet(line_mates() + [{S: 1 - lax.axis_index(S)}])
    else:
        greet(neighbours())
    for phase in range(3):
        ring.start(phase)
        if with_small:
            small.start(phase)
        ring.forward(phase)
        ring.finish(phase)
        if with_small:
            small.finish(phase)
    ring.settle()
    if with_small:
        small.settle()
        out[...] = small.sums[3]


def scattered(parts, cid, small=None):
    parts = [p.reshape((4, 2, 4, 2, 16, p.shape[-1])) for p in parts]
    widths = [p.shape[-1] for p in parts]
    vmem = pl.BlockSpec(memory_space=pltpu.VMEM)
    extra = [] if small is None else [small]
    scratch = scatter_scratch(widths) + [
        pltpu.SemaphoreType.DMA((54,)),
        pltpu.SemaphoreType.DMA((54,)),
        pltpu.SemaphoreType.DMA((27,)),
    ]
    if extra:
        rows = small.shape
        scratch += [
            pltpu.VMEM((4,) + rows, F32),
            pltpu.VMEM((8, 128), F32),
            pltpu.VMEM((9,) + rows, F32),
            pltpu.SemaphoreType.DMA((10,)),
            pltpu.SemaphoreType.DMA((10,)),
        ]
    return pl.pallas_call(
        functools.partial(scatter_kernel, bool(extra)),
        name="scatter",
        out_shape=[jax.ShapeDtypeStruct((16, w), F32) for w in widths]
        + [jax.ShapeDtypeStruct(e.shape, F32) for e in extra],
        in_specs=[ANY] * 3 + [vmem] * len(extra),
        out_specs=[vmem] * (3 + len(extra)),
        scratch_shapes=scratch,
        compiler_params=pltpu.CompilerParams(
            collective_id=cid, has_side_effects=True, vmem_limit_bytes=56 * MIB
        ),
    )(*parts, *extra)


def low(v):
    return v.astype(BF)


def matmul(left, right):
    return jnp.dot(left, right, preferred_element_type=F32)


def times_transposed(left, right):
    return lax.dot_general(left, right, (((1,), (1,)), ((), ())), preferred_element_type=F32)


def transposed_times(left, right):
    return lax.dot_general(left, right, (((0,), (0,)), ((), ())), preferred_element_type=F32)


def rms_norm(values, gain):
    return values * lax.rsqrt(jnp.mean(values * values, axis=-1, keepdims=True) + EPSILON) * gain


def rotate(values, cosine, sine):
    half = values.shape[-1] // 2
    a, b = values[..., :half], values[..., half:]
    return jnp.concatenate([a * cosine - b * sine, b * cosine + a * sine], -1)


def glu(gate, up):
    return jax.nn.silu(gate) * up


def swapped(value):
    return lax.ppermute(value, S, [(0, 1), (1, 0)])


def other_added(value):
    return value + swapped(value)


def joined(mine, axis):
    theirs = swapped(mine)
    first = lax.axis_index(S) == 0
    return jnp.concatenate([jnp.where(first, mine, theirs), jnp.where(first, theirs, mine)], axis)


def core_half(value, which, axis=1):
    size = value.shape[axis] // 2
    return lax.dynamic_slice_in_dim(value, which * size, size, axis)


def row_homes(turn):
    pairs = []
    for s in range(2):
        for i in range(64):
            core = (i % 2) ^ turn
            pairs.append((s * 64 + i, core * 64 + s * 32 + i // 2))
    return pairs


def mixer_halves(conv_in, qkv):
    def half(core):
        b = conv_in.reshape(8, 3, 2, 512)
        b = lax.dynamic_index_in_dim(b, core, 2, False).reshape(8, 1536)
        q = core_half(qkv[:, :1024], core)
        k = core_half(qkv[:, 1024:1536], core)
        v = core_half(qkv[:, 1536:], core)
        return jnp.concatenate([b, q, k, v], 1)

    odd = lax.axis_index(SQ) % 2
    got = [
        lax.ppermute(half(jnp.bitwise_xor(odd, turn)), (S, DP, SQ), row_homes(turn))
        for turn in range(2)
    ]
    first = lax.axis_index(S) == 0
    return jnp.concatenate([jnp.where(first, got[0], got[1]), jnp.where(first, got[1], got[0])], 0)


def mixer_homes(grads):
    core = lax.axis_index(S)
    got = []
    for turn in range(2):
        parity = jnp.bitwise_xor(core, turn)
        rows = lax.dynamic_slice_in_dim(grads, parity * 8, 8, 0)
        got.append(lax.ppermute(rows, (S, DP, SQ), [(b, a) for a, b in row_homes(turn)]))
    even = lax.axis_index(SQ) % 2 == 0
    lower = jnp.where(even, got[0], got[1])
    upper = jnp.where(even, got[1], got[0])
    both = jnp.stack([lower, upper], 1)
    conv = both[:, :, :1536].reshape(8, 2, 3, 512).transpose(0, 2, 1, 3).reshape(8, 3072)

    def side(start, stop):
        return both[:, :, start:stop].reshape(8, -1)

    return conv, jnp.concatenate([side(1536, 2048), side(2048, 2304), side(2304, 2560)], 1)


def to_heads(packed):
    width = packed.shape[1] // 4
    parts = packed.reshape(2, 128, 4, width).transpose(0, 2, 1, 3).reshape(8, 128, width)
    return lax.all_to_all(parts, SQ, 0, 0).reshape(1024, width)


def to_tokens(rows):
    width = rows.shape[1]
    parts = lax.all_to_all(rows.reshape(8, 128, width), SQ, 0, 0)
    return parts.reshape(2, 4, 128, width).transpose(0, 2, 1, 3).reshape(256, 4, width)


def rope_tables():
    positions = (lax.axis_index(SQ) * 128 + jnp.arange(128)).astype(F32)
    frequency = 1000000.0 ** (-jnp.arange(32).astype(F32) * 2.0 / 64)
    angles = positions[:, None] * frequency[None, :]
    tile = lambda t: jnp.concatenate([t, t], 0)[:, None, :]
    return tile(jnp.cos(angles)), tile(jnp.sin(angles))


def attention_probs(q, k):
    scores = jnp.einsum("qhd,kd->hqk", q, k, preferred_element_type=F32) * 0.125
    order = jnp.arange(1024)
    scores = jnp.where(order[:, None] >= order[None, :], scores, -1e9)
    return jax.nn.softmax(scores, axis=-1)


def attention(packed):
    q, k, v = packed[:, :128].reshape(1024, 2, 64), packed[:, 128:192], packed[:, 192:]
    probs = attention_probs(q, k)
    return jnp.einsum("hqk,kd->qhd", low(probs), v, preferred_element_type=F32).reshape(1024, 128)


def attention_back(packed, upstream):
    q, k, v = packed[:, :128].reshape(1024, 2, 64), packed[:, 128:192], packed[:, 192:]
    up = upstream.reshape(1024, 2, 64)
    probs = attention_probs(q, k)
    dv = jnp.einsum("hqk,qhd->kd", low(probs), up, preferred_element_type=F32)
    dp = jnp.einsum("qhd,kd->hqk", up, v, preferred_element_type=F32)
    ds = low(probs * (dp - jnp.sum(dp * probs, -1, keepdims=True)))
    dq = jnp.einsum("hqk,kd->qhd", ds, k, preferred_element_type=F32) * 0.125
    dk = jnp.einsum("hqk,qhd->kd", ds, q, preferred_element_type=F32) * 0.125
    return low(jnp.concatenate([dq.reshape(1024, 128), dk, dv], 1))


def ffn(hidden, gain, gate, up, down):
    normed = low(rms_norm(hidden, gain))
    g, u = matmul(normed, gate), matmul(normed, up)
    active = low(glu(g, u))
    return (normed, g, u, active), other_added(times_transposed(active, down))


def ffn_back(hidden, gain, gate, up, down, saved, upstream):
    normed, g, u, active = saved
    df = low(upstream)
    _, pull = jax.vjp(glu, g, u)
    dg, du = pull(matmul(df, down))
    dg, du = low(dg), low(du)
    d_normed = other_added(times_transposed(dg, gate) + times_transposed(du, up))
    _, pull = jax.vjp(rms_norm, hidden, gain)
    d_hidden, d_gain = pull(d_normed)
    grads = [low(transposed_times(a, b)) for a, b in ((normed, dg), (normed, du), (df, active))]
    return upstream + d_hidden, d_gain, grads


def shards(
    inputs,
    cotangent,
    conv_in,
    conv_kernel,
    qkv_weight,
    qk_gain,
    mix_gain,
    ffn_gain,
    mix_out,
    w_gate,
    w_up,
    w_down,
):
    core = lax.axis_index(S)
    first = core == 0
    x = inputs.reshape(256, 1024).astype(F32)
    cot = cotangent.reshape(256, 1024).astype(F32)
    gains = lax.all_gather(jnp.concatenate([mix_gain, ffn_gain], 0), S).astype(F32)
    qk = qk_gain.astype(F32)

    own = [mix_out[0], w_gate[0], w_up[0], w_down[0].T]
    keep = jnp.concatenate([core_half(w, core) for w in own], 1)
    got = swapped(jnp.concatenate([core_half(w, 1 - core) for w in own], 1))
    block0, block1 = jnp.where(first, keep, got), jnp.where(first, got, keep)
    cuts = (512, 2816, 5120)
    mo0, g0, u0, d0 = jnp.split(block0, cuts, 1)
    mo1, g1, u1, d1 = jnp.split(block1, cuts, 1)
    mixers = mixer_halves(conv_in, qkv_weight)
    ci, qw = mixers[:, :1536], mixers[:, 1536:]
    taps = jnp.pad(conv_kernel, ((0, 13), (0, 120)))
    early = [
        jnp.concatenate([g0, ci[:, :768], qw[:, :512]], 1),
        jnp.concatenate([u0, ci[:, 768:], qw[:, 512:]], 1),
        jnp.concatenate([d0, mo0, mo1, taps], 1),
    ]
    wide = [b.reshape(1024, -1) for b in gathered(early, 0)]
    late = [b.reshape(1024, -1) for b in gathered([g1, u1, d1], 1)]
    g0, u0, d0 = [w[:, :2304] for w in wide]
    g1, u1, d1 = late
    ci = jnp.concatenate([w[:, 2304:3072] for w in wide[:2]], 1)
    qw = jnp.concatenate([w[:, 3072:] for w in wide[:2]], 1)
    mo0 = joined(wide[2][:, 2304:2816], 1)
    mo1 = joined(wide[2][:, 2816:3328], 1)
    taps = wide[2][:, 3328:].reshape(64, 16, 128)[:, :3, :8].transpose(1, 0, 2).reshape(3, 512)
    taps = taps.astype(F32)

    n1 = low(rms_norm(x, gains[0, 0]))
    p1 = matmul(n1, ci)
    b_gate, c_gate, value = p1[:, :512], p1[:, 512:1024], p1[:, 1024:]
    bx = low(b_gate * value).reshape(2, 128, 512)
    rim = lax.ppermute(bx[:, 126:], SQ, [(i, i + 1) for i in range(7)])
    padded = jnp.concatenate([rim, bx], 1).astype(F32)
    conv = sum(taps[j] * padded[:, j : j + 128] for j in range(3)).reshape(256, 512)
    m1 = joined(low(c_gate * conv), 1)
    h1 = x + matmul(m1, mo0)
    saved0, f0 = ffn(h1, gains[0, 1], g0, u0, d0)
    z = low(h1 + f0).astype(F32)

    n2 = low(rms_norm(z, gains[1, 0]))
    p2 = matmul(n2, qw)
    cosine, sine = rope_tables()

    def head(raw, gain):
        return rotate(rms_norm(raw, gain), cosine, sine)

    q_raw, k_raw = p2[:, :512].reshape(256, 8, 64), p2[:, 512:768].reshape(256, 4, 64)
    q, q_pull = jax.vjp(head, q_raw, qk[0])
    k, k_pull = jax.vjp(head, k_raw, qk[1])
    packed = jnp.concatenate(
        [low(q).reshape(256, 4, 128), low(k), low(p2[:, 768:]).reshape(256, 4, 64)], 2
    )
    packed = to_heads(packed.reshape(256, 1024))
    att = to_tokens(low(attention(packed))).reshape(256, 512)
    att = joined(att, 1)
    h2 = z + matmul(att, mo1)
    saved1, f1 = ffn(h2, gains[1, 1], g1, u1, d1)
    result = low(h2 + f1)

    dh2, d_ffn1, late_grads = ffn_back(h2, gains[1, 1], g1, u1, d1, saved1, cot)
    late_sums = scattered(late_grads, 2)
    do2 = low(dh2)
    mo1_grad = low(transposed_times(att, core_half(do2, core)))
    d_att = low(times_transposed(do2, core_half(mo1, core, 0)))
    d_packed = to_tokens(attention_back(packed, to_heads(d_att))).astype(F32)
    dq_raw, dq_gain = q_pull(d_packed[:, :, :128].reshape(256, 8, 64))
    dk_raw, dk_gain = k_pull(d_packed[:, :, 128:192])
    dp2 = low(
        jnp.concatenate(
            [dq_raw.reshape(256, 512), dk_raw.reshape(256, 256), d_packed[:, :, 192:].reshape(256, 256)],
            1,
        )
    )
    qw_grad = low(transposed_times(n2, dp2))
    dn2 = other_added(times_transposed(dp2, qw))
    dz, d_mix1 = jax.vjp(rms_norm, z, gains[1, 0])[1](dn2)
    dz = low(dh2 + dz).astype(F32)

    dh1, d_ffn0, grads0 = ffn_back(h1, gains[0, 1], g0, u0, d0, saved0, dz)
    do1 = low(dh1)
    mo0_grad = low(transposed_times(m1, core_half(do1, core)))
    dm1 = times_transposed(do1, core_half(mo0, core, 0))
    dc = dm1 * conv
    dconv = (dm1 * c_gate).reshape(2, 128, 512)
    taps_grad = jnp.stack([jnp.sum(dconv * padded[:, j : j + 128], (0, 1)) for j in range(3)])
    d_padded = sum(jnp.pad(taps[j] * dconv, ((0, 0), (j, 2 - j), (0, 0))) for j in range(3))
    returned = lax.ppermute(d_padded[:, :2], SQ, [(i + 1, i) for i in range(7)])
    dbx = d_padded[:, 2:] + jnp.pad(returned, ((0, 0), (126, 0), (0, 0)))
    dbx = dbx.reshape(256, 512)
    dp1 = low(jnp.concatenate([dbx * value, dc, dbx * b_gate], 1))
    ci_grad = low(transposed_times(n1, dp1))
    dn1 = other_added(times_transposed(dp1, ci))
    dx, d_mix0 = jax.vjp(rms_norm, x, gains[0, 0])[1](dn1)
    input_grad = low(dh1 + dx)

    taps_grad = jnp.pad(taps_grad.reshape(3, 64, 8).transpose(1, 0, 2), ((0, 0), (0, 13), (0, 120)))
    parts = [
        jnp.concatenate([grads0[0], ci_grad[:, :768], qw_grad[:, :512]], 1),
        jnp.concatenate([grads0[1], ci_grad[:, 768:], qw_grad[:, 512:]], 1),
        jnp.concatenate([grads0[2], mo0_grad, mo1_grad, low(taps_grad.reshape(1024, 128))], 1),
    ]
    d_gains = jnp.stack([jnp.where(first, d_mix0, d_mix1), jnp.where(first, d_ffn0, d_ffn1)])
    d_qk = jnp.stack([dq_gain, dk_gain]).reshape(1, 128)
    small = jnp.concatenate([d_gains.reshape(16, 128), jnp.pad(d_qk, ((0, 7), (0, 0)))], 0)
    *sums, small = scattered(parts, 3, small)

    block0 = [sums[2][:, 2304:2816], sums[0][:, :2304], sums[1][:, :2304], sums[2][:, :2304]]
    block1 = [sums[2][:, 2816:3328]] + list(late_sums)
    block0, block1 = jnp.concatenate(block0, 1), jnp.concatenate(block1, 1)
    mine = jnp.where(first, block0, block1)
    theirs = swapped(jnp.where(first, block1, block0))
    lower = jnp.split(jnp.where(first, mine, theirs), cuts, 1)
    upper = jnp.split(jnp.where(first, theirs, mine), cuts, 1)
    mo_grad, g_grad, u_grad, d_grad = [jnp.concatenate(p, 1) for p in zip(lower, upper)]
    mixers = jnp.concatenate([sums[0][:, 2304:3072], sums[1][:, 2304:3072], sums[0][:, 3072:], sums[1][:, 3072:]], 1)
    conv_in_grad, qkv_grad = mixer_homes(mixers)
    return (
        core_half(result, core).reshape(2, 1, 128, 512),
        core_half(input_grad, core).reshape(2, 1, 128, 512),
        conv_in_grad,
        sums[2][:3, 3328:3336],
        qkv_grad,
        small[16].reshape(2, 64),
        small[:8].reshape(1, 1024),
        small[8:16].reshape(1, 1024),
        mo_grad[None],
        g_grad[None],
        u_grad[None],
        d_grad.T[None],
    )


def solution(mesh):
    every = (S, DP, SQ)
    weight = P(S, (DP, SQ), None)
    tokens = P(None, DP, SQ, None)
    in_specs = (
        tokens,
        tokens,
        P(every, None),
        P(None, every),
        P(every, None),
        P(),
        P(S, None),
        P(S, None),
        weight,
        weight,
        weight,
        P(S, None, (DP, SQ)),
    )
    tokens = P(None, DP, SQ, S)
    out_specs = (
        tokens,
        tokens,
        P(every, None),
        P(None, every),
        P(every, None),
        P(),
        P(S, None),
        P(S, None),
        weight,
        weight,
        weight,
        P(S, None, (DP, SQ)),
    )
    return jax.shard_map(shards, mesh=mesh, in_specs=in_specs, out_specs=out_specs, check_vma=False)
```

profile of v0, /device:TPU:25, one launch (start us, length us, event | category | flops | bytes accessed | tf_op | source)
XLA Modules:
  0.0 620.9 jit_solution(2622214588772974705)
XLA Ops:
  3.0 6.4 %collective-permute-start.2 = (bf16[8,2560]{1,0:T(8,128)(2,1)S(1)}, bf16[8,2560]{1,0:T(8,128)(2,1)S(1)}, u32[]{:S(2)}, u32[]{:S(2)}) collective-permute-start(bf16[8,2560]{1,0:T(8,128)(2,1)S(1)} %pad_maximum_fusion.39), channel_id=1, source_target_pairs={{0,64},{1,0},{2,65},{3,1},{4,66},{5,2},{6,67},{7,3},{8,68},{9,4},{... | collective-permute-start | bytes 122888 | tf_op jit(solution)/shard_map/ppermute | solution.py:461
  20.9 96.7 %gather.2 = (bf16[4,2,4,2,16,3584]{5,4,3,2,1,0:T(8,128)(2,1)}, bf16[4,2,4,2,16,3584]{5,4,3,2,1,0:T(8,128)(2,1)}, bf16[4,2,4,2,16,3456]{5,4,3,2,1,0:T(8,128)(2,1)}) custom-call(bf16[16,3584]{1,0:T(8,128)(2,1)} %pad_maximum_fusion.36.refs_0_, bf16[16,3584]{1,0:T(8,128)(2,1)} %fusion.86.refs_1_, bf16[16,3456]{1,0:T(8,128)(2,1)} %fusion.87.refs_2_), custom_call_target="tpu_custom_call" | custom-call | tf_op jit(solution)/shard_map/gather/pallas_call | solution.py:134
  119.9 4.1 collective-permute-start.8
  161.4 6.0 all-to-all-start
  167.7 8.3 %all-to-all-done = bf16[8,128,256]{2,1,0:T(8,128)(2,1)} async-done(((bf16[8,128,256]{2,1,0:T(8,128)(2,1)}), bf16[8,128,256]{2,1,0:T(8,128)(2,1)}, u32[]{:S(2)}, u32[]{:S(2)}) %all-to-all-start) | async-done | bytes 524320 | tf_op jit(solution)/shard_map/all_to_all | solution.py:490
  185.7 4.0 fusion.43
  190.6 5.7 all-to-all-start.1
  197.6 4.3 all-to-all-done.1
  206.8 66.7 %gather.3 = (bf16[4,2,4,2,16,2304]{5,4,3,2,1,0:T(8,128)(2,1)}, bf16[4,2,4,2,16,2304]{5,4,3,2,1,0:T(8,128)(2,1)}, bf16[4,2,4,2,16,2304]{5,4,3,2,1,0:T(8,128)(2,1)}) custom-call(bf16[16,2304]{1,0:T(8,128)(2,1)} %get-tuple-element.107.refs_0_, bf16[16,2304]{1,0:T(8,128)(2,1)} %get-tuple-element.106.refs_1_, bf16[16,2304]{1,0:T(8,128)(2,1)} %get-tuple-element.105.refs_2_), custom_call_target="tpu_custom_call" | custom-call | tf_op jit(solution)/shard_map/gather/pallas_call | solution.py:134
  301.2 5.4 all-to-all-start.2
  306.5 5.1 fusion.132
  317.3 7.2 %fusion.3 = (f32[2,1024]{1,0:T(2,128)S(1)}, f32[1024,1024,2]{1,0,2:T(8,128)S(1)}) fusion(f32[2,1024]{1,0:T(2,128)S(1)} %fusion.8, f32[2,1024]{1,0:T(2,128)S(1)} %get-tuple-element.155, f32[1024,1024,2]{1,0,2:T(8,128)} %copy-done, pred[1024,1024]{0,1:T(8,128)(4,1)} %copy-done.2, bf16[1024,2,64]{0,2,1:T(8,128)(2,1)} %reshape_reshape.8, ...), kind=kOutput, calls=%fused_computation.6 | convolution fusion | flops 281016320 | bytes 18374656 | tf_op jit(solution)/shard_map/qhd,kd->hqk/dot_general | solution.py:525
  324.5 5.0 fusion.5
  335.5 6.6 %all-to-all-start.3 = ((bf16[8,128,256]{1,2,0:T(8,128)(2,1)}), bf16[8,128,256]{1,2,0:T(8,128)(2,1)}, u32[]{:S(2)}, u32[]{:S(2)}) async-start(bf16[8,128,256]{1,2,0:T(8,128)(2,1)} %pad_maximum_fusion.20), calls=%async_computation.3 | async-start | bytes 1048576 | tf_op jit(solution)/shard_map/all_to_all | solution.py:495
  342.0 5.2 convolution_convert_fusion.2
  368.2 63.7 %scatter.3 = (f32[16,2304]{1,0:T(8,128)}, f32[16,2304]{1,0:T(8,128)}, f32[16,2304]{1,0:T(8,128)}) custom-call(bf16[4,2,4,2,16,2304]{5,4,3,2,1,0:T(8,128)(2,1)} %bitcast.304, bf16[4,2,4,2,16,2304]{5,4,3,2,1,0:T(8,128)(2,1)} %bitcast.305, bf16[4,2,4,2,16,2304]{5,4,3,2,1,0:T(8,128)(2,1)} %bitcast.309), custom_call_target="tpu_custom_call" | custom-call | tf_op jit(solution)/shard_map/scatter/pallas_call | solution.py:378
  449.9 4.1 collective-permute-start.12
  454.0 3.7 convolution_convert_fusion.5
  457.7 3.7 convolution_convert_fusion.4
  461.4 3.6 convolution_convert_fusion.3
  473.9 6.3 %pad_maximum_fusion.2 = bf16[1024,3456]{1,0:T(8,128)(2,1)} fusion(bf16[1024,128]{1,0:T(8,128)(2,1)S(1)} %bitcast.332, bf16[1024,512]{1,0:T(8,128)(2,1)} %convolution_convert_fusion.8, bf16[1024,512]{1,0:T(8,128)(2,1)} %convolution_convert_fusion.9, bf16[1024,2304]{1,0:T(8,128)(2,1)} %convolution_convert_fusion.3), kind=kLoop, calls=%fused_computation.14 | loop fusion | flops 28311552 | bytes 14155776 | tf_op jit(solution)/shard_map/concatenate | solution.py:671
  493.8 93.8 %scatter.2 = (f32[16,3584]{1,0:T(8,128)}, f32[16,3584]{1,0:T(8,128)}, f32[16,3456]{1,0:T(8,128)}, f32[24,128]{1,0:T(8,128)}) custom-call(bf16[4,2,4,2,16,3584]{5,4,3,2,1,0:T(8,128)(2,1)} %bitcast.306, bf16[4,2,4,2,16,3584]{5,4,3,2,1,0:T(8,128)(2,1)} %bitcast.307, bf16[4,2,4,2,16,3456]{5,4,3,2,1,0:T(8,128)(2,1)} %bitcast.308, ...), custom_call_target="tpu_custom_call" | custom-call | tf_op jit(solution)/shard_map/scatter/pallas_call | solution.py:378
  598.9 5.0 collective-permute-start.16
  611.0 4.4 collective-permute-done.15
  (489 shorter events, 193.3 us)
Async XLA Ops:
  0.6 123.3 %copy-start.4 = (bf16[2,1,128,1024]{3,2,1,0:T(8,128)(2,1)S(1)}, bf16[2,1,128,1024]{3,2,1,0:T(8,128)(2,1)}, u32[]{:S(2)}) copy-start(bf16[2,1,128,1024]{3,2,1,0:T(8,128)(2,1)} %param.12) | copy-start | bytes 1572868
  3.0 15.1 %collective-permute-start.2 = (bf16[8,2560]{1,0:T(8,128)(2,1)S(1)}, bf16[8,2560]{1,0:T(8,128)(2,1)S(1)}, u32[]{:S(2)}, u32[]{:S(2)}) collective-permute-start(bf16[8,2560]{1,0:T(8,128)(2,1)S(1)} %pad_maximum_fusion.39), channel_id=1, source_target_pairs={{0,64},{1,0},{2,65},{3,1},{4,66},{5,2},{6,67},{7,3},{8,68},{9,4},{... | collective-permute-start | bytes 122888 | tf_op jit(solution)/shard_map/ppermute | solution.py:461
  9.3 8.8 %collective-permute-start.1 = (bf16[8,2560]{1,0:T(8,128)(2,1)S(1)}, bf16[8,2560]{1,0:T(8,128)(2,1)S(1)}, u32[]{:S(2)}, u32[]{:S(2)}) collective-permute-start(bf16[8,2560]{1,0:T(8,128)(2,1)S(1)} %pad_maximum_fusion.38), channel_id=1, source_target_pairs={{0,0},{1,64},{2,1},{3,65},{4,2},{5,66},{6,3},{7,67},{8,4},{9,68},{... | collective-permute-start | bytes 122888 | tf_op jit(solution)/shard_map/ppermute | solution.py:461
  14.0 4.2 collective-permute-start
  119.9 13.9 %collective-permute-start.8 = (bf16[1024,512]{1,0:T(8,128)(2,1)}, bf16[1024,512]{1,0:T(8,128)(2,1)S(1)}, u32[]{:S(2)}, u32[]{:S(2)}) collective-permute-start(bf16[1024,512]{1,0:T(8,128)(2,1)} %slice.345), channel_id=1, source_target_pairs={{0,64},{64,0},{1,65},{65,1},{2,66},{66,2},{3,67},{67,3},{4,68},{68... | collective-permute-start | bytes 3145736 | tf_op jit(solution)/shard_map/ppermute | solution.py:423
  130.1 7.0 %collective-permute-start.3 = (bf16[2,2,512]{2,1,0:T(2,128)(2,1)S(1)}, bf16[2,2,512]{2,1,0:T(2,128)(2,1)S(1)}, u32[]{:S(2)}, u32[]{:S(2)}) collective-permute-start(bf16[2,2,512]{2,1,0:T(2,128)(2,1)S(1)} %slice.321), channel_id=1, source_target_pairs={{0,1},{1,2},{2,3},{3,4},{4,5},{5,6},{6,7},{8,9},{9,10},{10,11},{11... | collective-permute-start | bytes 12296 | tf_op jit(solution)/shard_map/ppermute | solution.py:603
  136.9 3.1 collective-permute-start.5
  137.6 2.3 collective-permute-start.4
  151.0 3.8 collective-permute-start.6
  161.4 14.6 %all-to-all-start = ((bf16[8,128,256]{2,1,0:T(8,128)(2,1)}), bf16[8,128,256]{2,1,0:T(8,128)(2,1)}, u32[]{:S(2)}, u32[]{:S(2)}) async-start(bf16[8,128,256]{2,1,0:T(8,128)(2,1)} %bitcast.31), calls=%async_computation | async-start | bytes 1048576 | tf_op jit(solution)/shard_map/all_to_all | solution.py:490
  190.6 11.3 %all-to-all-start.1 = ((bf16[8,128,128]{2,1,0:T(8,128)(2,1)}), bf16[8,128,128]{2,1,0:T(8,128)(2,1)S(1)}, u32[]{:S(2)}, u32[]{:S(2)}) async-start(bf16[8,128,128]{2,1,0:T(8,128)(2,1)} %copy.89), calls=%async_computation.1 | async-start | bytes 524288 | tf_op jit(solution)/shard_map/all_to_all | solution.py:495
  202.1 71.4 %collective-permute-start.7 = (bf16[256,512]{1,0:T(8,128)(2,1)S(1)}, bf16[256,512]{1,0:T(8,128)(2,1)S(1)}, u32[]{:S(2)}, u32[]{:S(2)}) collective-permute-start(bf16[256,512]{1,0:T(8,128)(2,1)S(1)} %bitcast.362), channel_id=1, source_target_pairs={{0,64},{64,0},{1,65},{65,1},{2,66},{66,2},{3,67},{67,3},{4,68},{68... | collective-permute-start | bytes 786440 | tf_op jit(solution)/shard_map/ppermute | solution.py:423
  286.6 6.8 %collective-permute-start.10 = (f32[256,1024]{1,0:T(8,128)S(1)}, f32[256,1024]{1,0:T(8,128)S(1)}, u32[]{:S(2)}, u32[]{:S(2)}) collective-permute-start(f32[256,1024]{1,0:T(8,128)S(1)} %convolution_add_fusion), channel_id=1, source_target_pairs={{0,64},{64,0},{1,65},{65,1},{2,66},{66,2},{3,67},{67,3},{4,68},{68... | collective-permute-start | bytes 3145736 | tf_op jit(solution)/shard_map/ppermute | solution.py:423
  301.2 10.8 %all-to-all-start.2 = ((bf16[8,128,128]{2,1,0:T(8,128)(2,1)}), bf16[8,128,128]{2,1,0:T(8,128)(2,1)}, u32[]{:S(2)}, u32[]{:S(2)}) async-start(bf16[8,128,128]{2,1,0:T(8,128)(2,1)} %bitcast.336), calls=%async_computation.2 | async-start | bytes 524288 | tf_op jit(solution)/shard_map/all_to_all | solution.py:490
  335.5 18.6 %all-to-all-start.3 = ((bf16[8,128,256]{1,2,0:T(8,128)(2,1)}), bf16[8,128,256]{1,2,0:T(8,128)(2,1)}, u32[]{:S(2)}, u32[]{:S(2)}) async-start(bf16[8,128,256]{1,2,0:T(8,128)(2,1)} %pad_maximum_fusion.20), calls=%async_computation.3 | async-start | bytes 1048576 | tf_op jit(solution)/shard_map/all_to_all | solution.py:495
  347.2 84.6 %collective-permute-start.9 = (f32[256,1024]{1,0:T(8,128)}, f32[256,1024]{1,0:T(8,128)}, u32[]{:S(2)}, u32[]{:S(2)}) collective-permute-start(f32[256,1024]{1,0:T(8,128)} %fusion.132), channel_id=1, source_target_pairs={{0,64},{64,0},{1,65},{65,1},{2,66},{66,2},{3,67},{67,3},{4,68},{68... | collective-permute-start | bytes 3145736 | tf_op jit(solution)/shard_map/ppermute | solution.py:423
  364.6 74.9 %collective-permute-start.11 = (f32[256,1024]{1,0:T(8,128)}, f32[256,1024]{1,0:T(8,128)}, u32[]{:S(2)}, u32[]{:S(2)}) collective-permute-start(f32[256,1024]{1,0:T(8,128)} %fusion.36), channel_id=1, source_target_pairs={{0,64},{64,0},{1,65},{65,1},{2,66},{66,2},{3,67},{67,3},{4,68},{68... | collective-permute-start | bytes 3145736 | tf_op jit(solution)/shard_map/ppermute | solution.py:423
  449.9 15.1 %collective-permute-start.12 = (f32[256,1024]{1,0:T(8,128)S(1)}, f32[256,1024]{1,0:T(8,128)S(1)}, u32[]{:S(2)}, u32[]{:S(2)}) collective-permute-start(f32[256,1024]{1,0:T(8,128)S(1)} %fusion.38), channel_id=1, source_target_pairs={{0,64},{64,0},{1,65},{65,1},{2,66},{66,2},{3,67},{67,3},{4,68},{68... | collective-permute-start | bytes 3145736 | tf_op jit(solution)/shard_map/ppermute | solution.py:423
  469.9 10.4 %collective-permute-start.13 = (f32[2,2,512]{2,1,0:T(2,128)S(1)}, f32[2,2,512]{2,1,0:T(2,128)S(1)}, u32[]{:S(2)}, u32[]{:S(2)}) collective-permute-start(f32[2,2,512]{2,1,0:T(2,128)S(1)} %pad_add_fusion.3), channel_id=1, source_target_pairs={{1,0},{2,1},{3,2},{4,3},{5,4},{6,5},{7,6},{9,8},{10,9},{11,10},{12... | collective-permute-start | bytes 24584 | tf_op jit(solution)/shard_map/ppermute | solution.py:658
  484.1 8.6 %collective-permute-start.14 = (f32[256,1024]{1,0:T(8,128)S(1)}, f32[256,1024]{1,0:T(8,128)S(1)}, u32[]{:S(2)}, u32[]{:S(2)}) collective-permute-start(f32[256,1024]{1,0:T(8,128)S(1)} %fusion.33), channel_id=1, source_target_pairs={{0,64},{64,0},{1,65},{65,1},{2,66},{66,2},{3,67},{67,3},{4,68},{68... | collective-permute-start | bytes 3145736 | tf_op jit(solution)/shard_map/ppermute | solution.py:423
  493.8 116.4 %copy-start.23 = (f32[256,1024]{1,0:T(8,128)S(1)}, f32[256,1024]{1,0:T(8,128)}, u32[]{:S(2)}) copy-start(f32[256,1024]{1,0:T(8,128)} %get-tuple-element.59) | copy-start | bytes 3145732
  598.9 12.1 %collective-permute-start.16 = (f32[8,2560]{1,0:T(8,128)}, f32[8,2560]{1,0:T(8,128)}, u32[]{:S(2)}, u32[]{:S(2)}) collective-permute-start(f32[8,2560]{1,0:T(8,128)} %get-tuple-element.117), channel_id=1, source_target_pairs={{64,0},{0,1},{65,2},{1,3},{66,4},{2,5},{67,6},{3,7},{68,8},{4,9},{... | collective-permute-start | bytes 245768 | tf_op jit(solution)/shard_map/ppermute | solution.py:474
  603.9 11.5 %collective-permute-start.15 = (f32[8,2560]{1,0:T(8,128)}, f32[8,2560]{1,0:T(8,128)}, u32[]{:S(2)}, u32[]{:S(2)}) collective-permute-start(f32[8,2560]{1,0:T(8,128)} %get-tuple-element.118), channel_id=1, source_target_pairs={{0,0},{64,1},{1,2},{65,3},{2,4},{66,5},{3,6},{67,7},{4,8},{68,9},{... | collective-permute-start | bytes 245768 | tf_op jit(solution)/shard_map/ppermute | solution.py:474
  608.1 9.5 %collective-permute-start.17 = (f32[16,7424]{1,0:T(8,128)S(1)}, f32[16,7424]{1,0:T(8,128)S(1)}, u32[]{:S(2)}, u32[]{:S(2)}) collective-permute-start(f32[16,7424]{1,0:T(8,128)S(1)} %fusion.72), channel_id=1, source_target_pairs={{0,64},{64,0},{1,65},{65,1},{2,66},{66,2},{3,67},{67,3},{4,68},{68... | collective-permute-start | bytes 1425416 | tf_op jit(solution)/shard_map/ppermute | solution.py:423
  (114 other events, 1367.4 us)
where the time goes:
time: 631 us; the launch traced here: 621 us
  Pallas kernels  321 us (51%)
  matrix products  82.3 us (13%)
  starting transfers between devices  66.9 us (11%)
  local copies, waits for them, and re-layouts  65.7 us (10%)
  other arithmetic  61.1 us (10%)
  waiting for transfers between devices  19.2 us (3%)
    pallas_call x2, Pallas kernels, gathered(): pl.pallas_call(gather_kernel, name='gather', out_shape=[jax.ShapeDtypeStr...  163 us
    pallas_call x2, Pallas kernels, scattered(): pl.pallas_call(functools.partial(scatter_kernel, bool(extra)), name='scat...  157 us
    dot_general x10, matrix products, transposed_times(): lax.dot_general(left, right, (((0,), (0,)), ((), ())), preferred_element_...  29.2 us
    ppermute x12, starting transfers between devices, swapped(): return lax.ppermute(value, S, [(0, 1), (1, 0)])  21.6 us
    dot_general x10, matrix products, matmul(): return jnp.dot(left, right, preferred_element_type=F32)  17.7 us
    convert_element_type x12, other arithmetic, low(): return v.astype(BF)  17.5 us
    dot_general x10, matrix products, times_transposed(): lax.dot_general(left, right, (((1,), (1,)), ((), ())), preferred_element_...  16.7 us
    unnamed x237, local copies, waits for them, and re-layouts  13.1 us
  transfers between devices with their start and end apart: 22, of which 5 were waited for; matrix products, arithmetic and copies ran while one was open for 15% of the time, Pallas kernels for 21%

commit v1 on v0

--- a/solution.py
+++ b/solution.py
@@ -389,6 +389,742 @@
     )(*parts, *extra)
 
 
+class Bag:
+    def __init__(self, **items):
+        self.__dict__.update(items)
+
+
+def launch(body, name, cid, ins, outs, scratch):
+    def kernel(*refs):
+        body(Bag(**dict(zip([*ins, *outs, *scratch], refs))))
+
+    got = pl.pallas_call(
+        kernel,
+        name=name,
+        out_shape=[jax.ShapeDtypeStruct(shape, dtype) for shape, dtype, _ in outs.values()],
+        in_specs=[where for _, where in ins.values()],
+        out_specs=[where for _, _, where in outs.values()],
+        scratch_shapes=list(scratch.values()),
+        compiler_params=pltpu.CompilerParams(
+            collective_id=cid, has_side_effects=True, vmem_limit_bytes=60 * MIB
+        ),
+    )(*[value for value, _ in ins.values()])
+    return Bag(**dict(zip(outs, got)))
+
+
+VM = pl.BlockSpec(memory_space=pltpu.VMEM)
+
+
+def vm(*shape, dtype=F32):
+    return pltpu.VMEM(shape, dtype)
+
+
+class Moves:
+    def __init__(self, local, send, recv):
+        self.sems = local, send, recv
+        self.kept, self.sent = [], []
+        self.locals = self.remotes = 0
+
+    def local(self, src, dst):
+        copy = pltpu.make_async_copy(src, dst, self.sems[0].at[self.locals])
+        self.locals += 1
+        copy.start()
+        return copy
+
+    def keep(self, src, dst):
+        self.kept.append(self.local(src, dst))
+
+    def remote(self, src, dst, device):
+        slot = self.remotes
+        self.remotes += 1
+        copy = pltpu.make_async_remote_copy(
+            src_ref=src,
+            dst_ref=dst,
+            send_sem=self.sems[1].at[slot],
+            recv_sem=self.sems[2].at[slot],
+            device_id=device,
+            device_id_type=MESH,
+        )
+        copy.start()
+        self.sent.append(copy)
+        return copy
+
+    def sibling(self, src, dst):
+        return self.remote(src, dst, {S: 1 - lax.axis_index(S)})
+
+    def mates(self, src, dst):
+        me = lax.axis_index(SQ)
+        copies = [self.remote(src(lax.rem(me + j, 8)), dst, {SQ: lax.rem(me + j, 8)}) for j in range(1, 8)]
+        return [self.local(src(me), dst)], copies
+
+    def done(self, copy):
+        copy.wait_send()
+        self.sent = [c for c in self.sent if c is not copy]
+
+    def flush(self):
+        for copy in self.kept:
+            copy.wait()
+        self.kept = []
+
+    def settle(self):
+        self.flush()
+        for copy in self.sent:
+            copy.wait_send()
+
+
+def arrived(moves):
+    own, copies = moves
+    for copy in own:
+        copy.wait()
+    for copy in copies:
+        copy.wait_recv()
+
+
+def mate_devices():
+    me = lax.axis_index(SQ)
+    return [{SQ: lax.rem(me + j, 8)} for j in range(1, 8)]
+
+
+def across_devices():
+    here = chip()
+    return [device_at(moved(here, axis, by)) for axis in range(2) for by in (1, -1)]
+
+
+def sibling_device():
+    return {S: 1 - lax.axis_index(S)}
+
+
+def by_rows(rows, step, size=32):
+    def body(i, carry):
+        step(pl.ds(pl.multiple_of(i * size, size), size))
+        return carry
+
+    lax.fori_loop(0, rows // size, body, 0)
+
+
+def by_columns(width, step, size=256):
+    def body(i, carry):
+        step(pl.ds(pl.multiple_of(i * size, size), size))
+        return carry
+
+    lax.fori_loop(0, width // size, body, 0)
+
+
+def core_columns(size):
+    return pl.ds(pl.multiple_of(lax.axis_index(S) * size, size), size)
+
+
+def inverse_norm(v):
+    return lax.rsqrt(jnp.mean(v * v, axis=-1, keepdims=True) + EPSILON)
+
+
+def norm_rows(src, gain, dst):
+    def step(rows):
+        v = src[rows].astype(F32)
+        dst[rows] = low(v * inverse_norm(v) * gain)
+
+    by_rows(256, step)
+
+
+def norm_back_rows(src, gain, upstreams, residual, out, d_gain):
+    d_gain[...] = jnp.zeros_like(d_gain)
+
+    def step(rows):
+        v = src[rows].astype(F32)
+        up = sum(u[rows] for u in upstreams)
+        r = inverse_norm(v)
+        t = up * gain
+        dv = r * (t - v * (r * r * jnp.mean(t * v, axis=-1, keepdims=True)))
+        out[rows] = (residual[rows].astype(F32) + dv).astype(out.dtype)
+        scaled = up * (v * r)
+        d_gain[...] += scaled[:8] + scaled[8:16] + scaled[16:24] + scaled[24:]
+
+    by_rows(256, step)
+
+
+def transpose_into(src, dst):
+    def step(cols):
+        dst[cols, :] = src[:, cols].astype(F32).T.astype(BF)
+
+    by_columns(1024, step, 128)
+
+
+def lanes(width=128):
+    return lax.broadcasted_iota(jnp.int32, (1, width), 1)
+
+
+def head_mean(v, ones):
+    return jnp.dot(v, ones, precision=lax.Precision.HIGHEST, preferred_element_type=F32)
+
+
+def half_turn(v):
+    return jnp.where(lanes() % 64 < 32, pltpu.roll(v, 96, 1), pltpu.roll(v, 32, 1))
+
+
+def head_lanes(v, head, upper):
+    v = v.astype(F32)
+    if head != upper:
+        v = pltpu.roll(v, 64, 1)
+    return jnp.where(lanes() >= 64 if upper else lanes() < 64, v, 0.0)
+
+
+def block_probs(b, block, head):
+    count = 256 * (block + 1)
+    q = head_lanes(b.packed[2 * block : 2 * block + 2, :, :128].reshape(256, 128), head, 0)
+    kv = b.packed[: 2 * block + 2, :, 128:].reshape(count, 128)
+    scores = times_transposed(low(q), kv) * 0.125
+    row = lax.broadcasted_iota(jnp.int32, (256, count), 0) + 256 * block
+    col = lax.broadcasted_iota(jnp.int32, (256, count), 1)
+    e = jnp.exp(jnp.where(row >= col, scores, -1e9))
+    return q, kv, e * (1.0 / jnp.sum(e, -1, keepdims=True))
+
+
+def forward_kernel(b):
+    core, seq = lax.axis_index(S), lax.axis_index(SQ)
+    greet(across_devices() + mate_devices() + [sibling_device()])
+    moves = Moves(b.local, b.send, b.recv)
+    here = chip()
+    shards, bufs = (b.gs, b.us, b.ds), (b.g1, b.u1, b.d1)
+    own = [moves.local(s, w.at[spot(here)]) for s, w in zip(shards, bufs)]
+    ci_loads = [
+        moves.local(w.at[:, pl.ds(2304, 768)], b.ci.at[:, pl.ds(i * 768, 768)])
+        for i, w in enumerate((b.w0, b.w1))
+    ]
+    for copy in own:
+        copy.wait()
+    ring = Gather(bufs, b.gsend, b.grecv)
+    ring.start(0)
+    half = core_columns(512)
+    mo_source = [b.w2.at[:, pl.ds(2304 + 512 * i, 512)] for i in range(2)]
+    mo_loads = [moves.local(s, d.at[:, half]) for s, d in zip(mo_source, (b.mo0, b.mo1))]
+    mo_swaps = [moves.sibling(s, d.at[:, half]) for s, d in zip(mo_source, (b.mo0, b.mo1))]
+    ffn_loads = [
+        moves.local(w.at[:, pl.ds(0, 2304)], d)
+        for w, d in ((b.w0, b.gate), (b.w1, b.up), (b.w2, b.down))
+    ]
+    qw_loads = [
+        moves.local(w.at[:, pl.ds(3072, 512)], b.qw.at[:, pl.ds(i * 512, 512)])
+        for i, w in enumerate((b.w0, b.w1))
+    ]
+    norm_rows(b.x, b.gains[0:1], b.normed)
+    for copy in ci_loads:
+        copy.wait()
+
+    def project(cols):
+        b.p1[:, cols] = matmul(b.normed[...], b.ci[:, cols])
+
+    by_columns(1536, project)
+    moves.keep(b.p1, b.p1_out)
+    ring.forward(0)
+
+    def gated(rows):
+        b.bx[rows] = low(b.p1[rows, :512] * b.p1[rows, 1024:]).astype(F32)
+
+    by_rows(256, gated)
+    for m in range(2):
+        b.pad[m, 8:] = b.bx[m * 128 : m * 128 + 128]
+    rim = moves.remote(b.pad.at[:, pl.ds(128, 8)], b.rim, {SQ: lax.rem(seq + 1, 8)})
+    ring.finish(0)
+    ring.start(1)
+    rim.wait_recv()
+    b.pad[:, :8] = jnp.where(seq > 0, b.rim[...], 0.0)
+    moves.keep(b.pad, b.pad_out)
+
+    def convolve(cols):
+        taps = b.taps[:, cols]
+        for m in range(2):
+            conv = sum(taps[j : j + 1] * b.pad[m, 6 + j : 134 + j, cols] for j in range(3))
+            rows = slice(m * 128, m * 128 + 128)
+            gate = b.p1[rows, pl.ds(pl.multiple_of(cols.start + 512, 128), 128)]
+            b.m1[rows, pl.ds(pl.multiple_of(core * 512 + cols.start, 128), 128)] = low(gate * conv)
+
+    by_columns(512, convolve, 128)
+    swap = moves.sibling(b.m1.at[:, half], b.m1.at[:, half])
+    ring.forward(1)
+    swap.wait_recv()
+    moves.keep(b.m1, b.m1_out)
+    for copy in mo_loads:
+        copy.wait()
+    for copy in mo_swaps:
+        copy.wait_recv()
+
+    def mix(cols):
+        b.h1[:, cols] = b.x[:, cols].astype(F32) + matmul(b.m1[...], b.mo0[:, cols])
+
+    by_columns(1024, mix)
+    moves.keep(b.h1, b.h1_out)
+    ring.finish(1)
+    ring.start(2)
+    norm_rows(b.h1, b.gains[1:2], b.normed)
+    for copy in ffn_loads:
+        copy.wait()
+
+    def hidden(cols):
+        g = matmul(b.normed[...], b.gate[:, cols])
+        u = matmul(b.normed[...], b.up[:, cols])
+        b.active[:, cols] = low(g / (1.0 + jnp.exp(-g)) * u)
+
+    by_columns(2304, hidden)
+
+    def contract(cols):
+        b.f[:, cols] = times_transposed(b.active[...], b.down[cols, :])
+
+    by_columns(1024, contract)
+    swap = moves.sibling(b.f, b.f_other)
+    ring.forward(2)
+    swap.wait_recv()
+
+    def passed(rows):
+        b.z[rows] = low(b.h1[rows] + (b.f[rows] + b.f_other[rows]))
+
+    by_rows(256, passed)
+    moves.keep(b.z, b.z_out)
+
+    norm_rows(b.z, b.gains[2:3], b.normed2)
+    for copy in qw_loads:
+        copy.wait()
+
+    def project2(cols):
+        b.p2[:, cols] = matmul(b.normed2[...], b.qw[:, cols])
+
+    by_columns(1024, project2)
+    moves.keep(b.p2, b.p2_out)
+    for chunk in range(8):
+        cols = slice(chunk * 128, chunk * 128 + 128)
+        head, place = chunk % 4, pl.ds(chunk // 4 * 128, 128)
+        for m in range(2):
+            v = b.p2[m * 128 : m * 128 + 128, cols]
+            y = v * lax.rsqrt(head_mean(v * v, b.ones[...]) + EPSILON) * b.qk[:, cols]
+            y = y * b.cosine[...] + half_turn(y) * b.sine[...]
+            if chunk >= 4:
+                y = jnp.where(lanes() < 64, y, v)
+            b.out[m * 4 + head, :, place] = low(y)
+    arrived(moves.mates(lambda j: b.out.at[j], b.packed.at[seq]))
+    moves.keep(b.packed, b.packed_out)
+    for block in range(4):
+        results = []
+        for head in range(2):
+            _, kv, probs = block_probs(b, block, head)
+            results.append(matmul(low(probs), kv))
+        joint = jnp.where(lanes() < 64, pltpu.roll(results[0], 64, 1), results[1])
+        b.att_rows[2 * block : 2 * block + 2] = low(joint).reshape(2, 128, 128)
+    rows = pl.ds(pl.multiple_of(seq // 4 * 128, 128), 128)
+    cols = pl.ds(pl.multiple_of(core * 512 + seq % 4 * 128, 128), 128)
+    arrived(moves.mates(lambda j: b.att_rows.at[j], b.att.at[rows, cols]))
+    swap = moves.sibling(b.att.at[:, half], b.att.at[:, half])
+    swap.wait_recv()
+    moves.keep(b.att, b.att_out)
+
+    def mix2(cols):
+        b.h2[:, cols] = b.z[:, cols].astype(F32) + matmul(b.att[...], b.mo1[:, cols])
+
+    by_columns(1024, mix2)
+    moves.keep(b.h2, b.h2_out)
+    moves.keep(b.mo0, b.mo0_out)
+    moves.keep(b.mo1, b.mo1_out)
+    ring.finish(2)
+    ring.settle()
+    moves.settle()
+
+
+def dma(count):
+    return pltpu.SemaphoreType.DMA((count,))
+
+
+def bf(*shape):
+    return pltpu.VMEM(shape, BF)
+
+
+def forward(x, gains, qk, cosine, sine, ones, taps, wide, late):
+    full = (4, 2, 4, 2, 16, 2304)
+    return launch(
+        forward_kernel,
+        "forward",
+        1,
+        dict(
+            x=(x, VM), gains=(gains, VM), qk=(qk, VM), cosine=(cosine, VM), sine=(sine, VM),
+            ones=(ones, VM), taps=(taps, VM), w0=(wide[0], ANY), w1=(wide[1], ANY), w2=(wide[2], ANY),
+            gs=(late[0], ANY), us=(late[1], ANY), ds=(late[2], ANY),
+        ),
+        dict(
+            g1=(full, BF, ANY), u1=(full, BF, ANY), d1=(full, BF, ANY),
+            p1_out=((256, 1536), F32, ANY), pad_out=((2, 136, 512), F32, ANY),
+            m1_out=((256, 1024), BF, ANY), h1_out=((256, 1024), F32, ANY), z_out=((256, 1024), BF, ANY),
+            p2_out=((256, 1024), F32, ANY), packed_out=((8, 128, 256), BF, ANY),
+            att_out=((256, 1024), BF, ANY), h2_out=((256, 1024), F32, ANY),
+            mo0_out=((1024, 1024), BF, ANY), mo1_out=((1024, 1024), BF, ANY),
+        ),
+        dict(
+            ci=bf(1024, 1536), qw=bf(1024, 1024), mo0=bf(1024, 1024), mo1=bf(1024, 1024),
+            gate=bf(1024, 2304), up=bf(1024, 2304), down=bf(1024, 2304),
+            normed=bf(256, 1024), normed2=bf(256, 1024), p1=vm(256, 1536), bx=vm(256, 512), pad=vm(2, 136, 512),
+            rim=vm(2, 8, 512), m1=bf(256, 1024), h1=vm(256, 1024), active=bf(256, 2304),
+            f=vm(256, 1024), f_other=vm(256, 1024), z=bf(256, 1024), p2=vm(256, 1024),
+            out=bf(8, 128, 256), packed=bf(8, 128, 256), att_rows=bf(8, 128, 128), att=bf(256, 1024),
+            h2=vm(256, 1024), local=dma(32), send=dma(24), recv=dma(24), gsend=dma(54), grecv=dma(54),
+        ),
+    )
+
+
+def ffn_scratch():
+    return dict(
+        wg=bf(2, 1024, 256), wu=bf(2, 1024, 256), wd=bf(2, 1024, 256),
+        sg=bf(2, 1024, 256), su=bf(2, 1024, 256), sd=bf(2, 1024, 256),
+        load=pltpu.SemaphoreType.DMA((2, 3)), store=pltpu.SemaphoreType.DMA((2, 3)),
+    )
+
+
+def ffn_loop(b, weights, grads, normed, normed_t, df, df_t, da, f=None):
+    def columns(i):
+        return pl.ds(pl.multiple_of(i * 256, 256), 256)
+
+    def loads(i, slot):
+        return [
+            pltpu.make_async_copy(w.at[:, columns(i)], d.at[slot], b.load.at[slot, k])
+            for k, (w, d) in enumerate(zip(weights, (b.wg, b.wu, b.wd)))
+        ]
+
+    def stores(i, slot):
+        return [
+            pltpu.make_async_copy(s.at[slot], g.at[:, columns(i)], b.store.at[slot, k])
+            for k, (g, s) in enumerate(zip(grads, (b.sg, b.su, b.sd)))
+        ]
+
+    for copy in loads(0, 0):
+        copy.start()
+    da[...] = jnp.zeros_like(da)
+    if f is not None:
+        f[...] = jnp.zeros_like(f)
+
+    def step(i, carry):
+        slot = lax.rem(i, 2)
+        for copy in loads(i, slot):
+            copy.wait()
+
+        @pl.when(i < 8)
+        def _():
+            for copy in loads(i + 1, 1 - slot):
+                copy.start()
+
+        gate, up, down = b.wg.at[slot], b.wu.at[slot], b.wd.at[slot]
+        g = matmul(normed[...], gate[...])
+        u = matmul(normed[...], up[...])
+        ds = matmul(df[...], down[...])
+        sig = 1.0 / (1.0 + jnp.exp(-g))
+        silu = g * sig
+        s = low(silu * u)
+        dg = low(ds * u * (sig * (1.0 + g * (1.0 - sig))))
+        du = low(ds * silu)
+        if f is not None:
+            f[...] += times_transposed(s, down[...])
+        da[...] += times_transposed(dg, gate[...]) + times_transposed(du, up[...])
+
+        @pl.when(i >= 2)
+        def _():
+            for copy in stores(i - 2, slot):
+                copy.wait()
+
+        b.sg[slot] = low(matmul(normed_t[...], dg))
+        b.su[slot] = low(matmul(normed_t[...], du))
+        b.sd[slot] = low(matmul(df_t[...], s))
+        for copy in stores(i, slot):
+            copy.start()
+        return carry
+
+    lax.fori_loop(0, 9, step, 0)
+    for copy in stores(7, 1) + stores(8, 0):
+        copy.wait()
+
+
+def middle_kernel(b):
+    greet([sibling_device()])
+    moves = Moves(b.local, b.send, b.recv)
+    norm_rows(b.h2, b.gains[3:4], b.normed)
+    transpose_into(b.normed, b.normed_t)
+    transpose_into(b.cot, b.cot_t)
+    ffn_loop(
+        b, (b.g1, b.u1, b.d1), (b.gg, b.gu, b.gd), b.normed, b.normed_t, b.cot, b.cot_t, b.da, b.f
+    )
+    half = core_columns(512)
+    other = pl.ds(pl.multiple_of(512 - lax.axis_index(S) * 512, 512), 512)
+    da_swap = moves.sibling(b.da, b.da_other)
+    f_swap = moves.sibling(b.f.at[:, other], b.f_other)
+    da_swap.wait_recv()
+    norm_back_rows(b.h2, b.gains[3:4], (b.da, b.da_other), b.cot, b.dh2, b.d_ffn)
+    f_swap.wait_recv()
+
+    def finish(rows):
+        b.result[rows] = low(b.h2[rows, half] + (b.f[rows, half] + b.f_other[rows]))
+
+    by_rows(256, finish)
+    moves.settle()
+
+
+def middle(h2, cot, gains, w):
+    grad = ((1024, 2304), BF, ANY)
+    return launch(
+        middle_kernel,
+        "middle",
+        2,
+        dict(
+            h2=(h2, VM), cot=(cot, VM), gains=(gains, VM),
+            g1=(w.g1.reshape(1024, 2304), ANY), u1=(w.u1.reshape(1024, 2304), ANY),
+            d1=(w.d1.reshape(1024, 2304), ANY),
+        ),
+        dict(
+            gg=grad, gu=grad, gd=grad, dh2=((256, 1024), F32, VM), d_ffn=((8, 1024), F32, VM),
+            result=((256, 512), BF, VM),
+        ),
+        dict(
+            normed=bf(256, 1024), normed_t=bf(1024, 256), cot_t=bf(1024, 256), da=vm(256, 1024),
+            da_other=vm(256, 1024), f=vm(256, 1024), f_other=vm(256, 512),
+            local=dma(2), send=dma(2), recv=dma(2), **ffn_scratch(),
+        ),
+    )
+
+
+def staged(moves, left_t, right, slots, dests):
+    for k, (slot, dest) in enumerate(zip(slots, dests)):
+        slot[...] = low(matmul(left_t[...], right(k)))
+        moves.keep(slot, dest)
+
+
+def backward_kernel(b):
+    core, seq = lax.axis_index(S), lax.axis_index(SQ)
+    greet(across_devices() + mate_devices() + [sibling_device()])
+    moves = Moves(b.local, b.send, b.recv)
+    ring = Scatter((b.rg, b.ru, b.rd), b.ring, (b.sum_g, b.sum_u, b.sum_d), b.ssend, b.srecv, b.sload)
+    ring.start(0)
+    half = core_columns(512)
+    mo1_load = moves.local(b.mo1_in, b.mo)
+    attn_loads = [
+        moves.local(w.at[:, pl.ds(3072, 512)], b.proj.at[:, pl.ds(i * 512, 512)])
+        for i, w in enumerate((b.w0, b.w1))
+    ]
+    packed_load = moves.local(b.packed_in, b.packed)
+    p2_load = moves.local(b.p2_in, b.p2)
+    p1_load = moves.local(b.p1_in, b.p1)
+
+    def rounded(rows):
+        b.do[rows] = low(b.dh2[rows])
+
+    by_rows(256, rounded)
+    mo1_load.wait()
+    first_row = pl.multiple_of(core * 512, 512)
+    for h in range(4):
+        rows = pl.ds(pl.multiple_of(first_row + h * 128, 128), 128)
+        d_att = low(times_transposed(b.do[...], b.mo[rows, :]))
+        for m in range(2):
+            b.out_att[m * 4 + h] = d_att[m * 128 : m * 128 + 128]
+    exchange = moves.mates(lambda j: b.out_att.at[j], b.d_att.at[seq])
+    transpose_into(b.att, b.turned)
+
+    def own_do(k):
+        return b.do[:, pl.ds(pl.multiple_of(core * 512 + k * 256, 256), 256)]
+
+    def places(grad, start, count):
+        return [grad.at[:, pl.ds(start + 256 * k, 256)] for k in range(count)]
+
+    def slots(*stacks):
+        return [stack.at[i] for stack in stacks for i in range(2)]
+
+    staged(moves, b.turned, own_do, slots(b.sg), places(b.grad2, 2816, 2))
+    mo0_load = moves.local(b.mo0_in, b.mo)
+    packed_load.wait()
+    arrived(exchange)
+    b.dkv[...] = jnp.zeros_like(b.dkv)
+    for block in range(4):
+        count = 256 * (block + 1)
+        results = []
+        for head in range(2):
+            q, kv, probs = block_probs(b, block, head)
+            up = low(head_lanes(b.d_att[2 * block : 2 * block + 2].reshape(256, 128), head, 1))
+            dp = times_transposed(up, kv)
+            ds = low(probs * (dp - jnp.sum(dp * probs, -1, keepdims=True)))
+            b.dkv[:count] += transposed_times(ds, low(q * 0.125)) + transposed_times(low(probs), up)
+            results.append(matmul(ds, kv) * 0.125)
+        joint = jnp.where(lanes() < 64, results[0], pltpu.roll(results[1], 64, 1))
+        b.out[2 * block : 2 * block + 2, :, :128] = low(joint).reshape(2, 128, 128)
+    for j in range(8):
+        b.out[j, :, 128:] = low(b.dkv[j * 128 : j * 128 + 128])
+    exchange = moves.mates(lambda j: b.out.at[j], b.d_packed.at[seq])
+    norm_rows(b.z, b.gains[2:3], b.normed)
+    transpose_into(b.normed, b.normed_t)
+    p2_load.wait()
+    arrived(exchange)
+    for chunk in range(8):
+        cols = slice(chunk * 128, chunk * 128 + 128)
+        head, place = chunk % 4, slice(chunk // 4 * 128, chunk // 4 * 128 + 128)
+        total = jnp.zeros((1, 128), F32)
+        for m in range(2):
+            v = b.p2[m * 128 : m * 128 + 128, cols]
+            up = b.d_packed[m * 4 + head, :, place].astype(F32)
+            r = lax.rsqrt(head_mean(v * v, b.ones[...]) + EPSILON)
+            dy = up * b.cosine[...] + half_turn(up * b.sine[...])
+            t = dy * b.qk[:, cols]
+            dv = r * (t - v * (r * r * head_mean(t * v, b.ones[...])))
+            total += jnp.sum(dy * (v * r), 0, keepdims=True)
+            if chunk >= 4:
+                dv = jnp.where(lanes() < 64, dv, up)
+            b.dp2[m * 128 : m * 128 + 128, cols] = low(dv)
+        b.d_qk[chunk : chunk + 1] = total
+    for copy in attn_loads:
+        copy.wait()
+
+    def back2(cols):
+        b.partial[:, cols] = times_transposed(b.dp2[...], b.proj[cols, :1024])
+
+    by_columns(1024, back2)
+    swap = moves.sibling(b.partial, b.other2)
+
+    ci_loads = [
+        moves.local(w.at[:, pl.ds(2304, 768)], b.proj.at[:, pl.ds(i * 768, 768)])
+        for i, w in enumerate((b.w0, b.w1))
+    ]
+    staged(
+        moves,
+        b.normed_t,
+        lambda k: b.dp2[:, k * 256 : k * 256 + 256],
+        slots(b.su, b.sd),
+        places(b.grad0, 3072, 2) + places(b.grad1, 3072, 2),
+    )
+    swap.wait_recv()
+    norm_back_rows(b.z, b.gains[2:3], (b.partial, b.other2), b.dh2, b.dz, b.d_mix1)
+    ring.forward(0)
+
+    norm_rows(b.h1, b.gains[1:2], b.normed)
+    transpose_into(b.normed, b.normed_t)
+    transpose_into(b.dz, b.turned)
+    moves.done(swap)
+    moves.flush()
+    ffn_loop(
+        b,
+        [w.at[:, pl.ds(0, 2304)] for w in (b.w0, b.w1, b.w2)],
+        [w.at[:, pl.ds(0, 2304)] for w in (b.grad0, b.grad1, b.grad2)],
+        b.normed, b.normed_t, b.dz, b.turned, b.partial,
+    )
+    swap = moves.sibling(b.partial, b.other0)
+    ring.finish(0)
+    ring.start(1)
+    swap.wait_recv()
+    norm_back_rows(b.h1, b.gains[1:2], (b.partial, b.other0), b.dz, b.dh1, b.d_ffn0)
+
+    def rounded0(rows):
+        b.do[rows] = low(b.dh1[rows])
+
+    by_rows(256, rounded0)
+    mo0_load.wait()
+    p1_load.wait()
+
+    def mixed(i, carry):
+        rows = pl.ds(pl.multiple_of(core * 512 + i * 128, 128), 128)
+        cols = pl.ds(pl.multiple_of(i * 128, 128), 128)
+        middle_cols = pl.ds(pl.multiple_of(512 + i * 128, 128), 128)
+        dm = times_transposed(b.do[...], b.mo[rows, :])
+        taps = b.taps[:, cols]
+        for m in range(2):
+            part = slice(m * 128, m * 128 + 128)
+            conv = sum(taps[j : j + 1] * b.pad[m, 6 + j : 134 + j, cols] for j in range(3))
+            b.dp1[part, middle_cols] = low(dm[part] * conv)
+            b.dconv[m, :128, cols] = dm[part] * b.p1[part, middle_cols]
+        return carry
+
+    lax.fori_loop(0, 4, mixed, 0)
+    rim = moves.remote(b.dconv.at[:, pl.ds(0, 8)], b.rim, {SQ: lax.rem(seq + 7, 8)})
+    transpose_into(b.m1, b.turned)
+    staged(moves, b.turned, own_do, slots(b.sg), places(b.grad2, 2304, 2))
+    norm_rows(b.x, b.gains[0:1], b.normed)
+    transpose_into(b.normed, b.normed_t)
+    ring.forward(1)
+    rim.wait_recv()
+    b.dconv[:, 128:] = jnp.where(seq < 7, b.rim[...], 0.0)
+    b.d_taps[...] = jnp.zeros_like(b.d_taps)
+
+    def conv_back(i, carry):
+        cols = pl.ds(pl.multiple_of(i * 128, 128), 128)
+        last_cols = pl.ds(pl.multiple_of(1024 + i * 128, 128), 128)
+        taps = b.taps[:, cols]
+        for m in range(2):
+            part = slice(m * 128, m * 128 + 128)
+            dconv = b.dconv[m, :128, cols]
+            for j in range(3):
+                b.d_taps[j : j + 1, cols] += jnp.sum(dconv * b.pad[m, 6 + j : 134 + j, cols], 0, keepdims=True)
+            dbx = sum(taps[2 - j : 3 - j] * b.dconv[m, j : 128 + j, cols] for j in range(3))
+            b.dp1[part, cols] = low(dbx * b.p1[part, last_cols])
+            b.dp1[part, last_cols] = low(dbx * b.p1[part, cols])
+        return carry
+
+    lax.fori_loop(0, 4, conv_back, 0)
+    for copy in ci_loads:
+        copy.wait()
+    moves.done(swap)
+
+    def back1(cols):
+        b.partial[:, cols] = times_transposed(b.dp1[...], b.proj[cols, :])
+
+    by_columns(1024, back1)
+    swap = moves.sibling(b.partial, b.other2)
+
+    staged(
+        moves,
+        b.normed_t,
+        lambda k: b.dp1[:, k * 256 : k * 256 + 256],
+        slots(b.su, b.sd, b.wg),
+        places(b.grad0, 2304, 3) + places(b.grad1, 2304, 3),
+    )
+    ring.finish(1)
+    ring.start(2)
+    swap.wait_recv()
+    norm_back_rows(b.x, b.gains[0:1], (b.partial, b.other2), b.dh1, b.dx, b.d_mix0)
+    ring.forward(2)
+    ring.finish(2)
+    ring.settle()
+    moves.settle()
+
+
+def backward(x, gains, qk, cosine, sine, ones, taps, wide, saved, mid):
+    full = (4, 2, 4, 2, 16, 2304)
+    partial_gain = ((8, 1024), F32, VM)
+    widths = (2304,) * 3
+    bufs = scatter_scratch(widths)
+    ring = {chr(97 + i // 9) + str(i % 9): s for i, s in enumerate(bufs)}
+
+    def body(b):
+        b.ring = [getattr(b, name) for name in ring]
+        backward_kernel(b)
+
+    return launch(
+        body,
+        "backward",
+        3,
+        dict(
+            x=(x, VM), gains=(gains, VM), qk=(qk, VM), cosine=(cosine, VM), sine=(sine, VM),
+            ones=(ones, VM), taps=(taps, VM), dh2=(mid.dh2, VM), att=(saved.att_out, VM), z=(saved.z_out, VM),
+            h1=(saved.h1_out, VM), m1=(saved.m1_out, VM), pad=(saved.pad_out, VM),
+            w0=(wide[0], ANY), w1=(wide[1], ANY), w2=(wide[2], ANY),
+            mo0_in=(saved.mo0_out, ANY), mo1_in=(saved.mo1_out, ANY), packed_in=(saved.packed_out, ANY),
+            p2_in=(saved.p2_out, ANY), p1_in=(saved.p1_out, ANY),
+            rg=(mid.gg.reshape(full), ANY), ru=(mid.gu.reshape(full), ANY), rd=(mid.gd.reshape(full), ANY),
+        ),
+        dict(
+            grad0=((1024, 3584), BF, ANY), grad1=((1024, 3584), BF, ANY), grad2=((1024, 3328), BF, ANY),
+            d_qk=((8, 128), F32, VM), d_mix1=partial_gain, d_ffn0=partial_gain, d_mix0=partial_gain,
+            d_taps=((8, 512), F32, VM), dx=((256, 1024), BF, VM),
+            sum_g=((16, 2304), F32, VM), sum_u=((16, 2304), F32, VM), sum_d=((16, 2304), F32, VM),
+        ),
+        dict(
+            mo=bf(1024, 1024), proj=bf(1024, 1536),
+            packed=bf(8, 128, 256), p2=vm(256, 1024), p1=vm(256, 1536), do=bf(256, 1024),
+            out_att=bf(8, 128, 128), d_att=bf(8, 128, 128), turned=bf(1024, 256), dkv=vm(1024, 128), out=bf(8, 128, 256),
+            d_packed=bf(8, 128, 256), normed=bf(256, 1024), normed_t=bf(1024, 256), dp2=bf(256, 1024),
+            partial=vm(256, 1024), other2=vm(256, 1024), other0=vm(256, 1024),
+            dz=bf(256, 1024), dh1=vm(256, 1024), dp1=bf(256, 1536), dconv=vm(2, 136, 512), rim=vm(2, 8, 512),
+            local=dma(32), send=dma(24), recv=dma(24), ssend=dma(54), srecv=dma(54), sload=dma(27),
+            **ffn_scratch(), **ring,
+        ),
+    )
+
+
 def low(v):
     return v.astype(BF)
 
@@ -405,32 +1141,8 @@
     return lax.dot_general(left, right, (((0,), (0,)), ((), ())), preferred_element_type=F32)
 
 
-def rms_norm(values, gain):
-    return values * lax.rsqrt(jnp.mean(values * values, axis=-1, keepdims=True) + EPSILON) * gain
-
-
-def rotate(values, cosine, sine):
-    half = values.shape[-1] // 2
-    a, b = values[..., :half], values[..., half:]
-    return jnp.concatenate([a * cosine - b * sine, b * cosine + a * sine], -1)
-
-
-def glu(gate, up):
-    return jax.nn.silu(gate) * up
-
-
 def swapped(value):
     return lax.ppermute(value, S, [(0, 1), (1, 0)])
-
-
-def other_added(value):
-    return value + swapped(value)
-
-
-def joined(mine, axis):
-    theirs = swapped(mine)
-    first = lax.axis_index(S) == 0
-    return jnp.concatenate([jnp.where(first, mine, theirs), jnp.where(first, theirs, mine)], axis)
 
 
 def core_half(value, which, axis=1):
@@ -452,9 +1164,9 @@
         b = conv_in.reshape(8, 3, 2, 512)
         b = lax.dynamic_index_in_dim(b, core, 2, False).reshape(8, 1536)
         q = core_half(qkv[:, :1024], core)
-        k = core_half(qkv[:, 1024:1536], core)
-        v = core_half(qkv[:, 1536:], core)
-        return jnp.concatenate([b, q, k, v], 1)
+        k = core_half(qkv[:, 1024:1536], core).reshape(8, 4, 64)
+        v = core_half(qkv[:, 1536:], core).reshape(8, 4, 64)
+        return jnp.concatenate([b, q, jnp.concatenate([k, v], 2).reshape(8, 512)], 1)
 
     odd = lax.axis_index(SQ) % 2
     got = [
@@ -478,75 +1190,16 @@
     both = jnp.stack([lower, upper], 1)
     conv = both[:, :, :1536].reshape(8, 2, 3, 512).transpose(0, 2, 1, 3).reshape(8, 3072)
 
-    def side(start, stop):
-        return both[:, :, start:stop].reshape(8, -1)
-
-    return conv, jnp.concatenate([side(1536, 2048), side(2048, 2304), side(2304, 2560)], 1)
-
-
-def to_heads(packed):
-    width = packed.shape[1] // 4
-    parts = packed.reshape(2, 128, 4, width).transpose(0, 2, 1, 3).reshape(8, 128, width)
-    return lax.all_to_all(parts, SQ, 0, 0).reshape(1024, width)
-
-
-def to_tokens(rows):
-    width = rows.shape[1]
-    parts = lax.all_to_all(rows.reshape(8, 128, width), SQ, 0, 0)
-    return parts.reshape(2, 4, 128, width).transpose(0, 2, 1, 3).reshape(256, 4, width)
+    kv = both[:, :, 2048:].reshape(8, 2, 4, 2, 64).transpose(0, 3, 1, 2, 4).reshape(8, 1024)
+    return conv, jnp.concatenate([both[:, :, 1536:2048].reshape(8, 1024), kv], 1)
 
 
 def rope_tables():
     positions = (lax.axis_index(SQ) * 128 + jnp.arange(128)).astype(F32)
     frequency = 1000000.0 ** (-jnp.arange(32).astype(F32) * 2.0 / 64)
     angles = positions[:, None] * frequency[None, :]
-    tile = lambda t: jnp.concatenate([t, t], 0)[:, None, :]
-    return tile(jnp.cos(angles)), tile(jnp.sin(angles))
-
-
-def attention_probs(q, k):
-    scores = jnp.einsum("qhd,kd->hqk", q, k, preferred_element_type=F32) * 0.125
-    order = jnp.arange(1024)
-    scores = jnp.where(order[:, None] >= order[None, :], scores, -1e9)
-    return jax.nn.softmax(scores, axis=-1)
-
-
-def attention(packed):
-    q, k, v = packed[:, :128].reshape(1024, 2, 64), packed[:, 128:192], packed[:, 192:]
-    probs = attention_probs(q, k)
-    return jnp.einsum("hqk,kd->qhd", low(probs), v, preferred_element_type=F32).reshape(1024, 128)
-
-
-def attention_back(packed, upstream):
-    q, k, v = packed[:, :128].reshape(1024, 2, 64), packed[:, 128:192], packed[:, 192:]
-    up = upstream.reshape(1024, 2, 64)
-    probs = attention_probs(q, k)
-    dv = jnp.einsum("hqk,qhd->kd", low(probs), up, preferred_element_type=F32)
-    dp = jnp.einsum("qhd,kd->hqk", up, v, preferred_element_type=F32)
-    ds = low(probs * (dp - jnp.sum(dp * probs, -1, keepdims=True)))
-    dq = jnp.einsum("hqk,kd->qhd", ds, k, preferred_element_type=F32) * 0.125
-    dk = jnp.einsum("hqk,qhd->kd", ds, q, preferred_element_type=F32) * 0.125
-    return low(jnp.concatenate([dq.reshape(1024, 128), dk, dv], 1))
-
-
-def ffn(hidden, gain, gate, up, down):
-    normed = low(rms_norm(hidden, gain))
-    g, u = matmul(normed, gate), matmul(normed, up)
-    active = low(glu(g, u))
-    return (normed, g, u, active), other_added(times_transposed(active, down))
-
-
-def ffn_back(hidden, gain, gate, up, down, saved, upstream):
-    normed, g, u, active = saved
-    df = low(upstream)
-    _, pull = jax.vjp(glu, g, u)
-    dg, du = pull(matmul(df, down))
-    dg, du = low(dg), low(du)
-    d_normed = other_added(times_transposed(dg, gate) + times_transposed(du, up))
-    _, pull = jax.vjp(rms_norm, hidden, gain)
-    d_hidden, d_gain = pull(d_normed)
-    grads = [low(transposed_times(a, b)) for a, b in ((normed, dg), (normed, du), (df, active))]
-    return upstream + d_hidden, d_gain, grads
+    cosine, sine = jnp.cos(angles), jnp.sin(angles)
+    return jnp.concatenate([cosine] * 4, 1), jnp.concatenate([-sine, sine] * 2, 1)
 
 
 def shards(
@@ -565,8 +1218,8 @@
 ):
     core = lax.axis_index(S)
     first = core == 0
-    x = inputs.reshape(256, 1024).astype(F32)
-    cot = cotangent.reshape(256, 1024).astype(F32)
+    x = inputs.reshape(256, 1024)
+    cot = cotangent.reshape(256, 1024)
     gains = lax.all_gather(jnp.concatenate([mix_gain, ffn_gain], 0), S).astype(F32)
     qk = qk_gain.astype(F32)
 
@@ -586,97 +1239,32 @@
         jnp.concatenate([d0, mo0, mo1, taps], 1),
     ]
     wide = [b.reshape(1024, -1) for b in gathered(early, 0)]
-    late = [b.reshape(1024, -1) for b in gathered([g1, u1, d1], 1)]
-    g0, u0, d0 = [w[:, :2304] for w in wide]
-    g1, u1, d1 = late
-    ci = jnp.concatenate([w[:, 2304:3072] for w in wide[:2]], 1)
-    qw = jnp.concatenate([w[:, 3072:] for w in wide[:2]], 1)
-    mo0 = joined(wide[2][:, 2304:2816], 1)
-    mo1 = joined(wide[2][:, 2816:3328], 1)
     taps = wide[2][:, 3328:].reshape(64, 16, 128)[:, :3, :8].transpose(1, 0, 2).reshape(3, 512)
-    taps = taps.astype(F32)
-
-    n1 = low(rms_norm(x, gains[0, 0]))
-    p1 = matmul(n1, ci)
-    b_gate, c_gate, value = p1[:, :512], p1[:, 512:1024], p1[:, 1024:]
-    bx = low(b_gate * value).reshape(2, 128, 512)
-    rim = lax.ppermute(bx[:, 126:], SQ, [(i, i + 1) for i in range(7)])
-    padded = jnp.concatenate([rim, bx], 1).astype(F32)
-    conv = sum(taps[j] * padded[:, j : j + 128] for j in range(3)).reshape(256, 512)
-    m1 = joined(low(c_gate * conv), 1)
-    h1 = x + matmul(m1, mo0)
-    saved0, f0 = ffn(h1, gains[0, 1], g0, u0, d0)
-    z = low(h1 + f0).astype(F32)
-
-    n2 = low(rms_norm(z, gains[1, 0]))
-    p2 = matmul(n2, qw)
+    taps = jnp.pad(taps.astype(F32), ((0, 5), (0, 0)))
+    gains = jnp.pad(jnp.stack([gains[0, 0], gains[0, 1], gains[1, 0], gains[1, 1]]), ((0, 4), (0, 0)))
+    kv_gain = jnp.concatenate([qk[1], jnp.ones((64,), F32)])
+    qk_row = jnp.concatenate([jnp.tile(qk[0], 8), jnp.tile(kv_gain, 4)])[None]
     cosine, sine = rope_tables()
-
-    def head(raw, gain):
-        return rotate(rms_norm(raw, gain), cosine, sine)
-
-    q_raw, k_raw = p2[:, :512].reshape(256, 8, 64), p2[:, 512:768].reshape(256, 4, 64)
-    q, q_pull = jax.vjp(head, q_raw, qk[0])
-    k, k_pull = jax.vjp(head, k_raw, qk[1])
-    packed = jnp.concatenate(
-        [low(q).reshape(256, 4, 128), low(k), low(p2[:, 768:]).reshape(256, 4, 64)], 2
-    )
-    packed = to_heads(packed.reshape(256, 1024))
-    att = to_tokens(low(attention(packed))).reshape(256, 512)
-    att = joined(att, 1)
-    h2 = z + matmul(att, mo1)
-    saved1, f1 = ffn(h2, gains[1, 1], g1, u1, d1)
-    result = low(h2 + f1)
-
-    dh2, d_ffn1, late_grads = ffn_back(h2, gains[1, 1], g1, u1, d1, saved1, cot)
-    late_sums = scattered(late_grads, 2)
-    do2 = low(dh2)
-    mo1_grad = low(transposed_times(att, core_half(do2, core)))
-    d_att = low(times_transposed(do2, core_half(mo1, core, 0)))
-    d_packed = to_tokens(attention_back(packed, to_heads(d_att))).astype(F32)
-    dq_raw, dq_gain = q_pull(d_packed[:, :, :128].reshape(256, 8, 64))
-    dk_raw, dk_gain = k_pull(d_packed[:, :, 128:192])
-    dp2 = low(
-        jnp.concatenate(
-            [dq_raw.reshape(256, 512), dk_raw.reshape(256, 256), d_packed[:, :, 192:].reshape(256, 256)],
-            1,
-        )
-    )
-    qw_grad = low(transposed_times(n2, dp2))
-    dn2 = other_added(times_transposed(dp2, qw))
-    dz, d_mix1 = jax.vjp(rms_norm, z, gains[1, 0])[1](dn2)
-    dz = low(dh2 + dz).astype(F32)
-
-    dh1, d_ffn0, grads0 = ffn_back(h1, gains[0, 1], g0, u0, d0, saved0, dz)
-    do1 = low(dh1)
-    mo0_grad = low(transposed_times(m1, core_half(do1, core)))
-    dm1 = times_transposed(do1, core_half(mo0, core, 0))
-    dc = dm1 * conv
-    dconv = (dm1 * c_gate).reshape(2, 128, 512)
-    taps_grad = jnp.stack([jnp.sum(dconv * padded[:, j : j + 128], (0, 1)) for j in range(3)])
-    d_padded = sum(jnp.pad(taps[j] * dconv, ((0, 0), (j, 2 - j), (0, 0))) for j in range(3))
-    returned = lax.ppermute(d_padded[:, :2], SQ, [(i + 1, i) for i in range(7)])
-    dbx = d_padded[:, 2:] + jnp.pad(returned, ((0, 0), (126, 0), (0, 0)))
-    dbx = dbx.reshape(256, 512)
-    dp1 = low(jnp.concatenate([dbx * value, dc, dbx * b_gate], 1))
-    ci_grad = low(transposed_times(n1, dp1))
-    dn1 = other_added(times_transposed(dp1, ci))
-    dx, d_mix0 = jax.vjp(rms_norm, x, gains[0, 0])[1](dn1)
-    input_grad = low(dh1 + dx)
-
-    taps_grad = jnp.pad(taps_grad.reshape(3, 64, 8).transpose(1, 0, 2), ((0, 0), (0, 13), (0, 120)))
-    parts = [
-        jnp.concatenate([grads0[0], ci_grad[:, :768], qw_grad[:, :512]], 1),
-        jnp.concatenate([grads0[1], ci_grad[:, 768:], qw_grad[:, 512:]], 1),
-        jnp.concatenate([grads0[2], mo0_grad, mo1_grad, low(taps_grad.reshape(1024, 128))], 1),
+    lane = jnp.arange(128)
+    ones = ((lane[:, None] // 64) == (lane[None, :] // 64)).astype(F32) / 64.0
+    common = (x, gains, qk_row, cosine, sine, ones, taps, wide)
+    saved = forward(*common, (g1, u1, d1))
+    mid = middle(saved.h2_out, cot, gains, saved)
+    back = backward(*common, saved, mid)
+
+    taps_grad = jnp.pad(back.d_taps[:3].reshape(3, 64, 8).transpose(1, 0, 2), ((0, 0), (0, 13), (0, 120)))
+    parts = [back.grad0, back.grad1, jnp.concatenate([back.grad2, low(taps_grad.reshape(1024, 128))], 1)]
+    d_mix0, d_ffn0, d_mix1, d_ffn1 = [
+        jnp.sum(g, 0) for g in (back.d_mix0, back.d_ffn0, back.d_mix1, mid.d_ffn)
     ]
     d_gains = jnp.stack([jnp.where(first, d_mix0, d_mix1), jnp.where(first, d_ffn0, d_ffn1)])
-    d_qk = jnp.stack([dq_gain, dk_gain]).reshape(1, 128)
+    d_q = jnp.sum(back.d_qk[:4].reshape(8, 64), 0)
+    d_qk = jnp.concatenate([d_q, jnp.sum(back.d_qk[4:, :64], 0)])[None]
     small = jnp.concatenate([d_gains.reshape(16, 128), jnp.pad(d_qk, ((0, 7), (0, 0)))], 0)
-    *sums, small = scattered(parts, 3, small)
+    *sums, small = scattered(parts, 4, small)
 
     block0 = [sums[2][:, 2304:2816], sums[0][:, :2304], sums[1][:, :2304], sums[2][:, :2304]]
-    block1 = [sums[2][:, 2816:3328]] + list(late_sums)
+    block1 = [sums[2][:, 2816:3328]] + [back.sum_g, back.sum_u, back.sum_d]
     block0, block1 = jnp.concatenate(block0, 1), jnp.concatenate(block1, 1)
     mine = jnp.where(first, block0, block1)
     theirs = swapped(jnp.where(first, block1, block0))
@@ -686,8 +1274,8 @@
     mixers = jnp.concatenate([sums[0][:, 2304:3072], sums[1][:, 2304:3072], sums[0][:, 3072:], sums[1][:, 3072:]], 1)
     conv_in_grad, qkv_grad = mixer_homes(mixers)
     return (
-        core_half(result, core).reshape(2, 1, 128, 512),
-        core_half(input_grad, core).reshape(2, 1, 128, 512),
+        mid.result.reshape(2, 1, 128, 512),
+        core_half(back.dx, core).reshape(2, 1, 128, 512),
         conv_in_grad,
         sums[2][:3, 3328:3336],
         qkv_grad,

time: 631 us -> 491 us (0.78)
  the two profiles are of different devices: /device:TPU:25 before, /device:TPU:1 now
where the time goes in v1:
time: 491 us; the launch traced here: 488 us
  Pallas kernels  422 us (86%)
  local copies, waits for them, and re-layouts  21.9 us (4%)
  other arithmetic  21.7 us (4%)
  starting transfers between devices  14.1 us (3%)
  waiting for transfers between devices  5.43 us (1%)
    pallas_call x3, Pallas kernels, launch(): pl.pallas_call(kernel, name=name, out_shape=[jax.ShapeDtypeStruct(shape,...  230 us
    pallas_call x1, Pallas kernels, gathered(): pl.pallas_call(gather_kernel, name='gather', out_shape=[jax.ShapeDtypeStr...  101 us
    pallas_call x1, Pallas kernels, scattered(): pl.pallas_call(functools.partial(scatter_kernel, bool(extra)), name='scat...  91.3 us
  transfers between devices with their start and end apart: 6, of which 2 were waited for; matrix products, arithmetic and copies ran while one was open for 2% of the time, Pallas kernels for 0%

profile of v1, /device:TPU:1, one launch (start us, length us, event | category | flops | bytes accessed | tf_op | source)
XLA Modules:
  0.0 487.7 jit_solution(6118199791218683332)
XLA Ops:
  0.7 0.9 dynamic-slice_bitcast_fusion.3
  1.6 1.0 dynamic-slice_bitcast_fusion.4
  3.4 1.5 collective-permute-start
  7.4 4.7 collective-permute-start.1
  12.3 1.0 collective-permute-start.2
  14.1 1.8 all-gather.1
  17.7 0.8 pad_maximum_fusion.7
  21.9 1.3 fusion.7.refs_2_
  23.3 100.6 %gather.1 = (bf16[4,2,4,2,16,3584]{5,4,3,2,1,0:T(8,128)(2,1)}, bf16[4,2,4,2,16,3584]{5,4,3,2,1,0:T(8,128)(2,1)}, bf16[4,2,4,2,16,3456]{5,4,3,2,1,0:T(8,128)(2,1)}) custom-call(bf16[16,3584]{1,0:T(8,128)(2,1)} %pad_maximum_fusion.6.refs_0_, bf16[16,3584]{1,0:T(8,128)(2,1)} %fusion.6.refs_1_, bf16[16,3456]{1,0:T(8,128)(2,1)} %fusion.7.refs_2_), custom_call_target="tpu_custom_call" | custom-call | tf_op jit(solution)/shard_map/gather/pallas_call | solution.py:134
  123.8 1.0 slice.156
  125.6 94.2 %forward.1 = (bf16[4,2,4,2,16,2304]{5,4,3,2,1,0:T(8,128)(2,1)}, bf16[4,2,4,2,16,2304]{5,4,3,2,1,0:T(8,128)(2,1)}, bf16[4,2,4,2,16,2304]{5,4,3,2,1,0:T(8,128)(2,1...) custom-call(bf16[256,1024]{1,0:T(8,128)(2,1)} %bitcast.122, ...), custom_call_target="tpu_custom_call" | custom-call | tf_op jit(solution)/shard_map/forward/pallas_call | solution.py:401
  219.8 26.8 %middle.1 = (bf16[1024,2304]{1,0:T(8,128)(2,1)}, bf16[1024,2304]{1,0:T(8,128)(2,1)}, bf16[1024,2304]{1,0:T(8,128)(2,1)}, f32[256,1024]{1,0:T(8,128)}, f32[8,1024]{1,0:T(8,128)}, /*index=5*/bf16[256,512]{1,0:T(8,128)(2,1)}) custom-call(f32[256,1024]{1,0:T(8,128)} %get-tuple-element.54.refs_0_, bf16[256,1024]{1,0:T(8,128)(2,1)} %bitcast.125, ...), custom_call_target="tpu_custom_call" | custom-call | tf_op jit(solution)/shard_map/middle/pallas_call | solution.py:401
  246.7 108.8 %backward.1 = (bf16[1024,3584]{1,0:T(8,128)(2,1)}, bf16[1024,3584]{1,0:T(8,128)(2,1)}, bf16[1024,3328]{1,0:T(8,128)(2,1)}, f32[8,128]{1,0:T(8,128)}, f32[8,1024]...) custom-call(bf16[256,1024]{1,0:T(8,128)(2,1)} %bitcast.123, ...), custom_call_target="tpu_custom_call" | custom-call | tf_op jit(solution)/shard_map/backward/pallas_call | solution.py:401
  361.0 6.3 %pad_maximum_fusion = bf16[1024,3456]{1,0:T(8,128)(2,1)} fusion(bf16[1024,128]{1,0:T(8,128)(2,1)S(1)} %bitcast.124, bf16[1024,3328]{1,0:T(8,128)(2,1)} %get-tuple-element.76), kind=kLoop, calls=%fused_computation | loop fusion | flops 14155776 | bytes 14155776 | tf_op jit(solution)/shard_map/concatenate | solution.py:1256
  367.3 91.3 %scatter.1 = (f32[16,3584]{1,0:T(8,128)}, f32[16,3584]{1,0:T(8,128)}, f32[16,3456]{1,0:T(8,128)}, f32[24,128]{1,0:T(8,128)}) custom-call(bf16[4,2,4,2,16,3584]{5,4,3,2,1,0:T(8,128)(2,1)} %bitcast.114, bf16[4,2,4,2,16,3584]{5,4,3,2,1,0:T(8,128)(2,1)} %bitcast.115, bf16[4,2,4,2,16,3456]{5,4,3,2,1,0:T(8,128)(2,1)} %bitcast.113, ...), custom_call_target="tpu_custom_call" | custom-call | tf_op jit(solution)/shard_map/scatter/pallas_call | solution.py:378
  458.6 1.0 slice.144
  460.4 0.9 slice.142
  462.1 0.9 slice.143
  465.3 1.3 slice.135
  466.6 1.3 fusion.20
  468.6 3.8 collective-permute-start.5
  472.5 3.0 collective-permute-start.3
  477.0 3.4 collective-permute-done.3
  480.4 2.0 collective-permute-done.4
  (111 shorter events, 27.0 us)
Async XLA Ops:
  3.4 16.4 %collective-permute-start = (bf16[16,7424]{1,0:T(8,128)(2,1)S(1)}, bf16[16,7424]{1,0:T(8,128)(2,1)S(1)}, u32[]{:S(2)}, u32[]{:S(2)}) collective-permute-start(bf16[16,7424]{1,0:T(8,128)(2,1)S(1)} %pad_maximum_fusion.4), channel_id=1, source_target_pairs={{0,64},{64,0},{1,65},{65,1},{2,66},{66,2},{3,67},{67,3},{4,68},{68... | collective-permute-start | bytes 712712 | tf_op jit(solution)/shard_map/ppermute | solution.py:1145
  7.4 12.3 %collective-permute-start.1 = (bf16[8,2560]{1,0:T(8,128)(2,1)S(1)}, bf16[8,2560]{1,0:T(8,128)(2,1)S(1)}, u32[]{:S(2)}, u32[]{:S(2)}) collective-permute-start(bf16[8,2560]{1,0:T(8,128)(2,1)S(1)} %pad_maximum_fusion.10), channel_id=1, source_target_pairs={{0,0},{1,64},{2,1},{3,65},{4,2},{5,66},{6,3},{7,67},{8,4},{9,68},{... | collective-permute-start | bytes 122888 | tf_op jit(solution)/shard_map/ppermute | solution.py:1173
  12.3 7.4 %collective-permute-start.2 = (bf16[8,2560]{1,0:T(8,128)(2,1)S(1)}, bf16[8,2560]{1,0:T(8,128)(2,1)S(1)}, u32[]{:S(2)}, u32[]{:S(2)}) collective-permute-start(bf16[8,2560]{1,0:T(8,128)(2,1)S(1)} %pad_maximum_fusion.11), channel_id=1, source_target_pairs={{0,64},{1,0},{2,65},{3,1},{4,66},{5,2},{6,67},{7,3},{8,68},{9,4},{... | collective-permute-start | bytes 122888 | tf_op jit(solution)/shard_map/ppermute | solution.py:1173
  246.6 112.5 %copy-start.5 = (f32[8,1024]{1,0:T(8,128)S(1)}, f32[8,1024]{1,0:T(8,128)}, u32[]{:S(2)}) copy-start(f32[8,1024]{1,0:T(8,128)} %get-tuple-element.81) | copy-start | bytes 98308
  367.2 101.3 %copy-start = (f32[16,2304]{1,0:T(8,128)S(1)}, f32[16,2304]{1,0:T(8,128)}, u32[]{:S(2)}) copy-start(f32[16,2304]{1,0:T(8,128)} %get-tuple-element.87) | copy-start | bytes 442372
  367.3 101.3 %copy-start.1 = (f32[16,2304]{1,0:T(8,128)S(1)}, f32[16,2304]{1,0:T(8,128)}, u32[]{:S(2)}) copy-start(f32[16,2304]{1,0:T(8,128)} %get-tuple-element.88) | copy-start | bytes 442372
  367.3 101.3 %copy-start.2 = (f32[16,2304]{1,0:T(8,128)S(1)}, f32[16,2304]{1,0:T(8,128)}, u32[]{:S(2)}) copy-start(f32[16,2304]{1,0:T(8,128)} %get-tuple-element.89) | copy-start | bytes 442372
  367.3 109.0 %copy-start.4 = (bf16[256,1024]{1,0:T(8,128)(2,1)S(1)}, bf16[256,1024]{1,0:T(8,128)(2,1)}, u32[]{:S(2)}) copy-start(bf16[256,1024]{1,0:T(8,128)(2,1)} %get-tuple-element.73) | copy-start | bytes 1572868
  458.6 28.4 %copy-start.3 = (bf16[256,512]{1,0:T(8,128)(2,1)S(1)}, bf16[256,512]{1,0:T(8,128)(2,1)}, u32[]{:S(2)}) copy-start(bf16[256,512]{1,0:T(8,128)(2,1)} %get-tuple-element.58) | copy-start | bytes 786436
  468.6 15.3 %collective-permute-start.5 = (f32[16,7424]{1,0:T(8,128)S(1)}, f32[16,7424]{1,0:T(8,128)S(1)}, u32[]{:S(2)}, u32[]{:S(2)}) collective-permute-start(f32[16,7424]{1,0:T(8,128)S(1)} %fusion), channel_id=1, source_target_pairs={{0,64},{64,0},{1,65},{65,1},{2,66},{66,2},{3,67},{67,3},{4,68},{68... | collective-permute-start | bytes 1425416 | tf_op jit(solution)/shard_map/ppermute | solution.py:1145
  472.5 7.9 %collective-permute-start.3 = (f32[8,2560]{1,0:T(8,128)S(1)}, f32[8,2560]{1,0:T(8,128)S(1)}, u32[]{:S(2)}, u32[]{:S(2)}) collective-permute-start(f32[8,2560]{1,0:T(8,128)S(1)} %get-tuple-element.161), channel_id=1, source_target_pairs={{0,0},{64,1},{1,2},{65,3},{2,4},{66,5},{3,6},{67,7},{4,8},{68,9},{... | collective-permute-start | bytes 245768 | tf_op jit(solution)/shard_map/ppermute | solution.py:1186
  475.5 6.9 %collective-permute-start.4 = (f32[8,2560]{1,0:T(8,128)S(1)}, f32[8,2560]{1,0:T(8,128)S(1)}, u32[]{:S(2)}, u32[]{:S(2)}) collective-permute-start(f32[8,2560]{1,0:T(8,128)S(1)} %get-tuple-element.160), channel_id=1, source_target_pairs={{64,0},{0,1},{65,2},{1,3},{66,4},{2,5},{67,6},{3,7},{68,8},{4,9},{... | collective-permute-start | bytes 245768 | tf_op jit(solution)/shard_map/ppermute | solution.py:1186

commit v2 on v1

--- a/solution.py
+++ b/solution.py
@@ -109,41 +109,6 @@
             for kind in range(6):
                 for colour in range(3):
                     self.copy(colour, phase, kind).wait_send()
-
-
-def gather_kernel(*refs):
-    shards, bufs, (own, send, recv) = refs[:3], refs[3:6], refs[6:]
-    here = chip()
-    greet(neighbours())
-    local = [
-        pltpu.make_async_copy(shards[c], bufs[c].at[spot(here)], own.at[c]) for c in range(3)
-    ]
-    for copy in local:
-        copy.start()
-    for copy in local:
-        copy.wait()
-    ring = Gather(bufs, send, recv)
-    for phase in range(3):
-        ring.start(phase)
-        ring.forward(phase)
-        ring.finish(phase)
-    ring.settle()
-
-
-def gathered(shards, cid):
-    return pl.pallas_call(
-        gather_kernel,
-        name="gather",
-        out_shape=[jax.ShapeDtypeStruct((4, 2, 4, 2) + s.shape, s.dtype) for s in shards],
-        in_specs=[ANY] * 3,
-        out_specs=[ANY] * 3,
-        scratch_shapes=[
-            pltpu.SemaphoreType.DMA((3,)),
-            pltpu.SemaphoreType.DMA((54,)),
-            pltpu.SemaphoreType.DMA((54,)),
-        ],
-        compiler_params=pltpu.CompilerParams(collective_id=cid, has_side_effects=True),
-    )(*shards)
 
 
 def lead(kept):
@@ -274,14 +239,14 @@
 
 
 class Small:
-    def __init__(self, value, sums, other, slots, send, recv):
-        self.value, self.sums, self.other, self.slots = value, sums, other, slots
+    def __init__(self, sums, other, slots, send, recv):
+        self.sums, self.other, self.slots = sums, other, slots
         self.send, self.recv = send, recv
         self.here = chip()
 
-    def sibling(self):
+    def sibling(self, source):
         return pltpu.make_async_remote_copy(
-            src_ref=self.value.at[pl.ds(16, 8)],
+            src_ref=source,
             dst_ref=self.other,
             send_sem=self.send.at[9],
             recv_sem=self.recv.at[9],
@@ -301,11 +266,6 @@
         )
 
     def start(self, phase):
-        if phase == 0:
-            self.sibling().start()
-            self.sibling().wait_recv()
-            self.sums[0] = self.value[...]
-            self.sums[0, 16:24] = self.value[16:24] + self.other[...]
         for by in (1, 2, 3):
             self.copy(phase, by).start()
 
@@ -316,77 +276,9 @@
         self.sums[phase + 1] = (self.sums[phase] + two) + (one + three)
 
     def settle(self):
-        self.sibling().wait_send()
         for phase in range(3):
             for by in (1, 2, 3):
                 self.copy(phase, by).wait_send()
-
-
-def line_mates():
-    here = chip()
-    return [device_at(moved(here, axis, by)) for axis in range(3) for by in (1, 2, 3)]
-
-
-def scatter_kernel(with_small, *refs):
-    refs = list(refs)
-    parts = [refs.pop(0) for _ in range(3)]
-    value = refs.pop(0) if with_small else None
-    results = [refs.pop(0) for _ in range(3)]
-    out = refs.pop(0) if with_small else None
-    bufs, refs = refs[:63], refs[63:]
-    send, recv, load = refs[:3]
-    ring = Scatter(parts, bufs, results, send, recv, load)
-    if with_small:
-        sums, other, slots, ssend, srecv = refs[3:]
-        small = Small(value, sums, other, slots, ssend, srecv)
-        greet(line_mates() + [{S: 1 - lax.axis_index(S)}])
-    else:
-        greet(neighbours())
-    for phase in range(3):
-        ring.start(phase)
-        if with_small:
-            small.start(phase)
-        ring.forward(phase)
-        ring.finish(phase)
-        if with_small:
-            small.finish(phase)
-    ring.settle()
-    if with_small:
-        small.settle()
-        out[...] = small.sums[3]
-
-
-def scattered(parts, cid, small=None):
-    parts = [p.reshape((4, 2, 4, 2, 16, p.shape[-1])) for p in parts]
-    widths = [p.shape[-1] for p in parts]
-    vmem = pl.BlockSpec(memory_space=pltpu.VMEM)
-    extra = [] if small is None else [small]
-    scratch = scatter_scratch(widths) + [
-        pltpu.SemaphoreType.DMA((54,)),
-        pltpu.SemaphoreType.DMA((54,)),
-        pltpu.SemaphoreType.DMA((27,)),
-    ]
-    if extra:
-        rows = small.shape
-        scratch += [
-            pltpu.VMEM((4,) + rows, F32),
-            pltpu.VMEM((8, 128), F32),
-            pltpu.VMEM((9,) + rows, F32),
-            pltpu.SemaphoreType.DMA((10,)),
-            pltpu.SemaphoreType.DMA((10,)),
-        ]
-    return pl.pallas_call(
-        functools.partial(scatter_kernel, bool(extra)),
-        name="scatter",
-        out_shape=[jax.ShapeDtypeStruct((16, w), F32) for w in widths]
-        + [jax.ShapeDtypeStruct(e.shape, F32) for e in extra],
-        in_specs=[ANY] * 3 + [vmem] * len(extra),
-        out_specs=[vmem] * (3 + len(extra)),
-        scratch_shapes=scratch,
-        compiler_params=pltpu.CompilerParams(
-            collective_id=cid, has_side_effects=True, vmem_limit_bytes=56 * MIB
-        ),
-    )(*parts, *extra)
 
 
 class Bag:
@@ -521,7 +413,7 @@
 def norm_rows(src, gain, dst):
     def step(rows):
         v = src[rows].astype(F32)
-        dst[rows] = low(v * inverse_norm(v) * gain)
+        dst[rows] = low(v * inverse_norm(v) * gain[...])
 
     by_rows(256, step)
 
@@ -533,7 +425,7 @@
         v = src[rows].astype(F32)
         up = sum(u[rows] for u in upstreams)
         r = inverse_norm(v)
-        t = up * gain
+        t = up * gain[...]
         dv = r * (t - v * (r * r * jnp.mean(t * v, axis=-1, keepdims=True)))
         out[rows] = (residual[rows].astype(F32) + dv).astype(out.dtype)
         scaled = up * (v * r)
@@ -579,43 +471,124 @@
     return q, kv, e * (1.0 / jnp.sum(e, -1, keepdims=True))
 
 
+def flat(value):
+    return value.reshape(-1, value.shape[-1])
+
+
+def ring_shape(width):
+    return (4, 2, 4, 2, 16, width)
+
+
 def forward_kernel(b):
     core, seq = lax.axis_index(S), lax.axis_index(SQ)
     greet(across_devices() + mate_devices() + [sibling_device()])
     moves = Moves(b.local, b.send, b.recv)
-    here = chip()
-    shards, bufs = (b.gs, b.us, b.ds), (b.g1, b.u1, b.d1)
-    own = [moves.local(s, w.at[spot(here)]) for s, w in zip(shards, bufs)]
-    ci_loads = [
-        moves.local(w.at[:, pl.ds(2304, 768)], b.ci.at[:, pl.ds(i * 768, 768)])
-        for i, w in enumerate((b.w0, b.w1))
+    here = spot(chip())
+    half, other_half = core_columns(512), pl.ds(pl.multiple_of(512 - core * 512, 512), 512)
+
+    mine = pl.ds(pl.multiple_of(core * 8, 8), 8)
+    waits = [
+        moves.local(b.mix_in.at[core], b.mix.at[mine]),
+        moves.local(b.gains_in, b.gains.at[core]),
+        moves.local(b.taps_in, b.mt.at[here + (slice(None), pl.ds(512, 128))]),
     ]
-    for copy in own:
+    swaps = [
+        moves.sibling(b.mix_in.at[1 - core], b.mix.at[mine]),
+        moves.sibling(b.gains_in, b.gains.at[core]),
+    ]
+    shards = (
+        (b.wg, 2304, (b.gate0, b.gate1)),
+        (b.wu, 2304, (b.up0, b.up1)),
+        (b.wd, 2304, (b.down0, b.down1)),
+        (b.mo, 512, (b.mt, b.mo1)),
+    )
+
+    def trade(k, block):
+        w, n, homes = shards[k]
+        home = homes[block].at[here + (slice(None), pl.ds(0, n))]
+        keep = pltpu.make_async_copy(w.at[:, pl.ds(block * n, n)], home, b.trade.at[k])
+        give = pltpu.make_async_remote_copy(
+            src_ref=w.at[:, pl.ds((1 - block) * n, n)],
+            dst_ref=home,
+            send_sem=b.trade.at[4 + k],
+            recv_sem=b.trade.at[8 + k],
+            device_id=sibling_device(),
+            device_id_type=MESH,
+        )
+        return keep, give
+
+    for block in range(2):
+
+        @pl.when(core == block)
+        def _():
+            for k in (3, 0, 1, 2):
+                for copy in trade(k, block):
+                    copy.start()
+
+    perm_load = moves.local(b.perm_in, b.perm)
+    for copy in waits:
         copy.wait()
-    ring = Gather(bufs, b.gsend, b.grecv)
-    ring.start(0)
-    half = core_columns(512)
-    mo_source = [b.w2.at[:, pl.ds(2304 + 512 * i, 512)] for i in range(2)]
-    mo_loads = [moves.local(s, d.at[:, half]) for s, d in zip(mo_source, (b.mo0, b.mo1))]
-    mo_swaps = [moves.sibling(s, d.at[:, half]) for s, d in zip(mo_source, (b.mo0, b.mo1))]
-    ffn_loads = [
-        moves.local(w.at[:, pl.ds(0, 2304)], d)
-        for w, d in ((b.w0, b.gate), (b.w1, b.up), (b.w2, b.down))
+    for copy in swaps:
+        copy.wait_recv()
+    b.ci0[here] = low(b.mix[:, :768])
+    b.ci1[here] = low(b.mix[:, 768:1536])
+    b.qw0[here] = low(b.mix[:, 1536:2048])
+    b.qw1[here] = low(b.mix[:, 2048:])
+    for k in (3, 0, 1, 2):
+        keep, give = trade(k, 0)
+        keep.wait()
+        give.wait_recv()
+    moves.keep(b.gains, b.gains_out)
+
+    rings = [
+        Gather(bufs, b.gsend.at[i], b.grecv.at[i])
+        for i, bufs in enumerate(
+            (
+                (b.ci0, b.ci1, b.mt),
+                (b.gate0, b.up0, b.down0),
+                (b.qw0, b.qw1, b.mo1),
+                (b.gate1, b.up1, b.down1),
+            )
+        )
     ]
-    qw_loads = [
-        moves.local(w.at[:, pl.ds(3072, 512)], b.qw.at[:, pl.ds(i * 512, 512)])
-        for i, w in enumerate((b.w0, b.w1))
-    ]
-    norm_rows(b.x, b.gains[0:1], b.normed)
-    for copy in ci_loads:
-        copy.wait()
-
-    def project(cols):
-        b.p1[:, cols] = matmul(b.normed[...], b.ci[:, cols])
-
-    by_columns(1536, project)
+    ring_a, ring_b, ring_c, ring_d = rings
+    for ring in rings:
+        ring.start(0)
+    norm_rows(b.x, b.gains.at[0, 0:1], b.normed)
+    perm_load.wait()
+    permuted(b.normed, b.perm, b.turned)
+    for ring in rings:
+        ring.forward(0)
+    ring_a.finish(0)
+    ring_a.start(1)
+    ring_b.finish(0)
+    ring_b.start(1)
+    ring_a.forward(1)
+    ring_a.finish(1)
+    ring_a.start(2)
+    ring_b.forward(1)
+    ring_c.finish(0)
+    ring_c.start(1)
+    ring_a.forward(2)
+    ring_b.finish(1)
+    ring_b.start(2)
+    ring_a.finish(2)
+
+    def other_mo(source, target):
+        return moves.sibling(source.at[..., pl.ds(0, 512)], target)
+
+    mo0_swap = other_mo(b.mt, b.mo0_other)
+    ring_d.finish(0)
+    ring_d.start(1)
+    for x in range(4):
+        rows = flat(b.mt[x, :, :, :, :, 512:]).reshape(16, 16, 128)
+        b.taps[:, x * 128 : x * 128 + 128] = jnp.sum(rows.astype(F32), 0)[:8]
+    for i, ci in enumerate((b.ci0, b.ci1)):
+        for j in range(3):
+            cols = slice(j * 256, j * 256 + 256)
+            b.p1[:, i * 768 + j * 256 : i * 768 + j * 256 + 256] = matmul(b.turned[...], flat(ci[..., cols]))
     moves.keep(b.p1, b.p1_out)
-    ring.forward(0)
+    ring_c.forward(1)
 
     def gated(rows):
         b.bx[rows] = low(b.p1[rows, :512] * b.p1[rows, 1024:]).astype(F32)
@@ -624,8 +597,9 @@
     for m in range(2):
         b.pad[m, 8:] = b.bx[m * 128 : m * 128 + 128]
     rim = moves.remote(b.pad.at[:, pl.ds(128, 8)], b.rim, {SQ: lax.rem(seq + 1, 8)})
-    ring.finish(0)
-    ring.start(1)
+    ring_c.finish(1)
+    ring_c.start(2)
+    ring_d.forward(1)
     rim.wait_recv()
     b.pad[:, :8] = jnp.where(seq > 0, b.rim[...], 0.0)
     moves.keep(b.pad, b.pad_out)
@@ -640,38 +614,36 @@
 
     by_columns(512, convolve, 128)
     swap = moves.sibling(b.m1.at[:, half], b.m1.at[:, half])
-    ring.forward(1)
+    ring_b.forward(2)
+    ring_d.finish(1)
     swap.wait_recv()
     moves.keep(b.m1, b.m1_out)
-    for copy in mo_loads:
-        copy.wait()
-    for copy in mo_swaps:
-        copy.wait_recv()
-
-    def mix(cols):
-        b.h1[:, cols] = b.x[:, cols].astype(F32) + matmul(b.m1[...], b.mo0[:, cols])
-
-    by_columns(1024, mix)
+    moves.keep(b.taps, b.taps_out)
+    mo0_swap.wait_recv()
+    b.h1[:, half] = b.x[:, half].astype(F32) + matmul(b.m1[...], flat(b.mt[..., :512]))
+    b.h1[:, other_half] = b.x[:, other_half].astype(F32) + matmul(b.m1[...], flat(b.mo0_other[...]))
     moves.keep(b.h1, b.h1_out)
-    ring.finish(1)
-    ring.start(2)
-    norm_rows(b.h1, b.gains[1:2], b.normed)
-    for copy in ffn_loads:
-        copy.wait()
+    norm_rows(b.h1, b.gains.at[0, 1:2], b.normed)
+    ring_b.finish(2)
+    ring_d.start(2)
+    ring_c.forward(2)
 
     def hidden(cols):
-        g = matmul(b.normed[...], b.gate[:, cols])
-        u = matmul(b.normed[...], b.up[:, cols])
+        g = matmul(b.normed[...], flat(b.gate0[..., cols]))
+        u = matmul(b.normed[...], flat(b.up0[..., cols]))
         b.active[:, cols] = low(g / (1.0 + jnp.exp(-g)) * u)
 
     by_columns(2304, hidden)
 
-    def contract(cols):
-        b.f[:, cols] = times_transposed(b.active[...], b.down[cols, :])
-
-    by_columns(1024, contract)
+    def contract(x, carry):
+        cols = pl.ds(pl.multiple_of(x * 256, 256), 256)
+        b.f[:, cols] = times_transposed(b.active[...], flat(b.down0[x]))
+        return carry
+
+    lax.fori_loop(0, 4, contract, 0)
     swap = moves.sibling(b.f, b.f_other)
-    ring.forward(2)
+    ring_c.finish(2)
+    mo1_swap = other_mo(b.mo1, b.mo1_other)
     swap.wait_recv()
 
     def passed(rows):
@@ -680,14 +652,12 @@
     by_rows(256, passed)
     moves.keep(b.z, b.z_out)
 
-    norm_rows(b.z, b.gains[2:3], b.normed2)
-    for copy in qw_loads:
-        copy.wait()
-
-    def project2(cols):
-        b.p2[:, cols] = matmul(b.normed2[...], b.qw[:, cols])
-
-    by_columns(1024, project2)
+    norm_rows(b.z, b.gains.at[1, 0:1], b.normed)
+    permuted(b.normed, b.perm, b.turned)
+    for i, qw in enumerate((b.qw0, b.qw1)):
+        for j in range(2):
+            cols = slice(j * 256, j * 256 + 256)
+            b.p2[:, i * 512 + j * 256 : i * 512 + j * 256 + 256] = matmul(b.turned[...], flat(qw[..., cols]))
     moves.keep(b.p2, b.p2_out)
     for chunk in range(8):
         cols = slice(chunk * 128, chunk * 128 + 128)
@@ -699,8 +669,15 @@
             if chunk >= 4:
                 y = jnp.where(lanes() < 64, y, v)
             b.out[m * 4 + head, :, place] = low(y)
-    arrived(moves.mates(lambda j: b.out.at[j], b.packed.at[seq]))
+    exchange = moves.mates(lambda j: b.out.at[j], b.packed.at[seq])
+    for ring_out, ref in (
+        (b.ci0_out, b.ci0), (b.ci1_out, b.ci1), (b.gate0_out, b.gate0), (b.up0_out, b.up0),
+        (b.down0_out, b.down0), (b.qw0_out, b.qw0), (b.qw1_out, b.qw1),
+    ):
+        moves.keep(ref, ring_out)
+    arrived(exchange)
     moves.keep(b.packed, b.packed_out)
+    ring_d.forward(2)
     for block in range(4):
         results = []
         for head in range(2):
@@ -710,58 +687,78 @@
         b.att_rows[2 * block : 2 * block + 2] = low(joint).reshape(2, 128, 128)
     rows = pl.ds(pl.multiple_of(seq // 4 * 128, 128), 128)
     cols = pl.ds(pl.multiple_of(core * 512 + seq % 4 * 128, 128), 128)
-    arrived(moves.mates(lambda j: b.att_rows.at[j], b.att.at[rows, cols]))
+    exchange = moves.mates(lambda j: b.att_rows.at[j], b.att.at[rows, cols])
+    mo1_swap.wait_recv()
+    for out, own, other in ((b.mo0_out, b.mt, b.mo0_other), (b.mo1_out, b.mo1, b.mo1_other)):
+        moves.keep(own.at[..., pl.ds(0, 512)], out.at[..., half])
+        moves.keep(other, out.at[..., other_half])
+    arrived(exchange)
     swap = moves.sibling(b.att.at[:, half], b.att.at[:, half])
     swap.wait_recv()
     moves.keep(b.att, b.att_out)
-
-    def mix2(cols):
-        b.h2[:, cols] = b.z[:, cols].astype(F32) + matmul(b.att[...], b.mo1[:, cols])
-
-    by_columns(1024, mix2)
+    b.h2[:, half] = b.z[:, half].astype(F32) + matmul(b.att[...], flat(b.mo1[...]))
+    b.h2[:, other_half] = b.z[:, other_half].astype(F32) + matmul(b.att[...], flat(b.mo1_other[...]))
     moves.keep(b.h2, b.h2_out)
-    moves.keep(b.mo0, b.mo0_out)
-    moves.keep(b.mo1, b.mo1_out)
-    ring.finish(2)
-    ring.settle()
+    ring_d.finish(2)
+    for ring in rings:
+        ring.settle()
+    for k in range(4):
+        trade(k, 0)[1].wait_send()
     moves.settle()
 
 
-def dma(count):
-    return pltpu.SemaphoreType.DMA((count,))
+def permuted(src, perm, dst):
+    def step(cols):
+        dst[:, cols] = low(matmul(src[...], perm[:, cols]))
+
+    by_columns(1024, step)
+
+
+def dma(*count):
+    return pltpu.SemaphoreType.DMA(count)
 
 
 def bf(*shape):
     return pltpu.VMEM(shape, BF)
 
 
-def forward(x, gains, qk, cosine, sine, ones, taps, wide, late):
-    full = (4, 2, 4, 2, 16, 2304)
+def forward(x, gains_in, qk, cosine, sine, ones, perm, taps, mix_in, weights):
+    def saved(*shape, dtype=BF):
+        return (shape, dtype, ANY)
+
+    wide, thin = ring_shape(2304), ring_shape(512)
+    wg, wu, wd, mo = weights
     return launch(
         forward_kernel,
         "forward",
         1,
         dict(
-            x=(x, VM), gains=(gains, VM), qk=(qk, VM), cosine=(cosine, VM), sine=(sine, VM),
-            ones=(ones, VM), taps=(taps, VM), w0=(wide[0], ANY), w1=(wide[1], ANY), w2=(wide[2], ANY),
-            gs=(late[0], ANY), us=(late[1], ANY), ds=(late[2], ANY),
+            x=(x, VM), gains_in=(gains_in, VM), qk=(qk, VM), cosine=(cosine, VM), sine=(sine, VM), ones=(ones, VM),
+            perm_in=(perm, ANY), taps_in=(taps, VM), mix_in=(mix_in, VM),
+            wg=(wg, ANY), wu=(wu, ANY), wd=(wd, ANY), mo=(mo, ANY),
         ),
         dict(
-            g1=(full, BF, ANY), u1=(full, BF, ANY), d1=(full, BF, ANY),
-            p1_out=((256, 1536), F32, ANY), pad_out=((2, 136, 512), F32, ANY),
-            m1_out=((256, 1024), BF, ANY), h1_out=((256, 1024), F32, ANY), z_out=((256, 1024), BF, ANY),
-            p2_out=((256, 1024), F32, ANY), packed_out=((8, 128, 256), BF, ANY),
-            att_out=((256, 1024), BF, ANY), h2_out=((256, 1024), F32, ANY),
-            mo0_out=((1024, 1024), BF, ANY), mo1_out=((1024, 1024), BF, ANY),
+            gate1=saved(*wide), up1=saved(*wide), down1=saved(*wide), ci0_out=saved(*ring_shape(768)),
+            ci1_out=saved(*ring_shape(768)), gate0_out=saved(*wide), up0_out=saved(*wide),
+            down0_out=saved(*wide), qw0_out=saved(*thin), qw1_out=saved(*thin),
+            mo0_out=saved(*ring_shape(1024)), mo1_out=saved(*ring_shape(1024)),
+            gains_out=saved(2, 8, 1024, dtype=F32), taps_out=saved(8, 512, dtype=F32),
+            p1_out=saved(256, 1536, dtype=F32), pad_out=saved(2, 136, 512, dtype=F32),
+            m1_out=saved(256, 1024), h1_out=saved(256, 1024, dtype=F32), z_out=saved(256, 1024),
+            p2_out=saved(256, 1024, dtype=F32), packed_out=saved(8, 128, 256),
+            att_out=saved(256, 1024), h2_out=saved(256, 1024, dtype=F32),
         ),
         dict(
-            ci=bf(1024, 1536), qw=bf(1024, 1024), mo0=bf(1024, 1024), mo1=bf(1024, 1024),
-            gate=bf(1024, 2304), up=bf(1024, 2304), down=bf(1024, 2304),
-            normed=bf(256, 1024), normed2=bf(256, 1024), p1=vm(256, 1536), bx=vm(256, 512), pad=vm(2, 136, 512),
+            mix=vm(16, 2560), gains=vm(2, 8, 1024), taps=vm(8, 512), perm=bf(1024, 1024),
+            ci0=bf(*ring_shape(768)), ci1=bf(*ring_shape(768)), mt=bf(*ring_shape(640)),
+            gate0=bf(*wide), up0=bf(*wide), down0=bf(*wide), qw0=bf(*thin), qw1=bf(*thin), mo1=bf(*thin),
+            mo0_other=bf(*thin), mo1_other=bf(*thin),
+            normed=bf(256, 1024), turned=bf(256, 1024), p1=vm(256, 1536), bx=vm(256, 512), pad=vm(2, 136, 512),
             rim=vm(2, 8, 512), m1=bf(256, 1024), h1=vm(256, 1024), active=bf(256, 2304),
             f=vm(256, 1024), f_other=vm(256, 1024), z=bf(256, 1024), p2=vm(256, 1024),
             out=bf(8, 128, 256), packed=bf(8, 128, 256), att_rows=bf(8, 128, 128), att=bf(256, 1024),
-            h2=vm(256, 1024), local=dma(32), send=dma(24), recv=dma(24), gsend=dma(54), grecv=dma(54),
+            h2=vm(256, 1024), local=dma(40), send=dma(28), recv=dma(28), trade=dma(12),
+            gsend=dma(4, 54), grecv=dma(4, 54),
         ),
     )
 
@@ -839,7 +836,7 @@
 def middle_kernel(b):
     greet([sibling_device()])
     moves = Moves(b.local, b.send, b.recv)
-    norm_rows(b.h2, b.gains[3:4], b.normed)
+    norm_rows(b.h2, b.gains.at[1, 1:2], b.normed)
     transpose_into(b.normed, b.normed_t)
     transpose_into(b.cot, b.cot_t)
     ffn_loop(
@@ -850,7 +847,7 @@
     da_swap = moves.sibling(b.da, b.da_other)
     f_swap = moves.sibling(b.f.at[:, other], b.f_other)
     da_swap.wait_recv()
-    norm_back_rows(b.h2, b.gains[3:4], (b.da, b.da_other), b.cot, b.dh2, b.d_ffn)
+    norm_back_rows(b.h2, b.gains.at[1, 1:2], (b.da, b.da_other), b.cot, b.dh2, b.d_ffn)
     f_swap.wait_recv()
 
     def finish(rows):
@@ -860,16 +857,15 @@
     moves.settle()
 
 
-def middle(h2, cot, gains, w):
+def middle(cot, w):
     grad = ((1024, 2304), BF, ANY)
     return launch(
         middle_kernel,
         "middle",
         2,
         dict(
-            h2=(h2, VM), cot=(cot, VM), gains=(gains, VM),
-            g1=(w.g1.reshape(1024, 2304), ANY), u1=(w.u1.reshape(1024, 2304), ANY),
-            d1=(w.d1.reshape(1024, 2304), ANY),
+            h2=(w.h2_out, VM), cot=(cot, VM), gains=(w.gains_out, VM),
+            g1=(flat(w.gate1), ANY), u1=(flat(w.up1), ANY), d1=(flat(w.down1), ANY),
         ),
         dict(
             gg=grad, gu=grad, gd=grad, dh2=((256, 1024), F32, VM), d_ffn=((8, 1024), F32, VM),
@@ -889,48 +885,63 @@
         moves.keep(slot, dest)
 
 
+def slots(*stacks):
+    return [stack.at[i] for stack in stacks for i in range(2)]
+
+
+def places(grad, count):
+    return [grad.at[:, pl.ds(256 * k, 256)] for k in range(count)]
+
+
+def unpermuted(b, mine, theirs, out):
+    def step(cols):
+        total = mine[:, cols] + theirs[:, cols]
+        high = low(total)
+        b.high[:, cols] = high
+        b.rest[:, cols] = low(total - high.astype(F32))
+
+    by_columns(1024, step)
+
+    def turn(cols):
+        out[:, cols] = times_transposed(b.high[...], b.perm[cols, :]) + times_transposed(b.rest[...], b.perm[cols, :])
+
+    by_columns(1024, turn)
+
+
 def backward_kernel(b):
     core, seq = lax.axis_index(S), lax.axis_index(SQ)
     greet(across_devices() + mate_devices() + [sibling_device()])
     moves = Moves(b.local, b.send, b.recv)
-    ring = Scatter((b.rg, b.ru, b.rd), b.ring, (b.sum_g, b.sum_u, b.sum_d), b.ssend, b.srecv, b.sload)
+    ring = Scatter((b.rg, b.ru, b.rd), b.ring, (b.sum_g, b.sum_u, b.sum_d), b.ssend.at[0], b.srecv.at[0], b.sload.at[0])
+    blocks = [g.reshape(ring_shape(512)) for g in (b.qw0_grad, b.qw1_grad, b.mo1_grad)]
+    ring2 = Scatter(blocks, b.ring2, (b.sum_q0, b.sum_q1, b.sum_mo), b.ssend.at[1], b.srecv.at[1], b.sload.at[1])
     ring.start(0)
-    half = core_columns(512)
     mo1_load = moves.local(b.mo1_in, b.mo)
+    packed_load = moves.local(b.packed_in, b.packed)
     attn_loads = [
-        moves.local(w.at[:, pl.ds(3072, 512)], b.proj.at[:, pl.ds(i * 512, 512)])
-        for i, w in enumerate((b.w0, b.w1))
+        moves.local(w, b.proj.at[:, pl.ds(i * 512, 512)]) for i, w in enumerate((b.qw0, b.qw1))
     ]
-    packed_load = moves.local(b.packed_in, b.packed)
     p2_load = moves.local(b.p2_in, b.p2)
-    p1_load = moves.local(b.p1_in, b.p1)
+    perm_load = moves.local(b.perm_in, b.perm)
 
     def rounded(rows):
         b.do[rows] = low(b.dh2[rows])
 
     by_rows(256, rounded)
     mo1_load.wait()
-    first_row = pl.multiple_of(core * 512, 512)
     for h in range(4):
-        rows = pl.ds(pl.multiple_of(first_row + h * 128, 128), 128)
+        rows = pl.ds(pl.multiple_of(core * 512 + h * 128, 128), 128)
         d_att = low(times_transposed(b.do[...], b.mo[rows, :]))
         for m in range(2):
             b.out_att[m * 4 + h] = d_att[m * 128 : m * 128 + 128]
     exchange = moves.mates(lambda j: b.out_att.at[j], b.d_att.at[seq])
     transpose_into(b.att, b.turned)
-
-    def own_do(k):
-        return b.do[:, pl.ds(pl.multiple_of(core * 512 + k * 256, 256), 256)]
-
-    def places(grad, start, count):
-        return [grad.at[:, pl.ds(start + 256 * k, 256)] for k in range(count)]
-
-    def slots(*stacks):
-        return [stack.at[i] for stack in stacks for i in range(2)]
-
-    staged(moves, b.turned, own_do, slots(b.sg), places(b.grad2, 2816, 2))
-    mo0_load = moves.local(b.mo0_in, b.mo)
+    staged(moves, b.turned, lambda k: own_columns(b.do, k), slots(b.sg), places(b.mo1_grad, 2))
     packed_load.wait()
+    norm_rows(b.z, b.gains.at[1, 0:1], b.normed)
+    perm_load.wait()
+    permuted(b.normed, b.perm, b.high)
+    transpose_into(b.high, b.normed_t)
     arrived(exchange)
     b.dkv[...] = jnp.zeros_like(b.dkv)
     for block in range(4):
@@ -948,14 +959,13 @@
     for j in range(8):
         b.out[j, :, 128:] = low(b.dkv[j * 128 : j * 128 + 128])
     exchange = moves.mates(lambda j: b.out.at[j], b.d_packed.at[seq])
-    norm_rows(b.z, b.gains[2:3], b.normed)
-    transpose_into(b.normed, b.normed_t)
+    ring.forward(0)
     p2_load.wait()
     arrived(exchange)
+    b.d_qk[...] = jnp.zeros_like(b.d_qk)
     for chunk in range(8):
         cols = slice(chunk * 128, chunk * 128 + 128)
         head, place = chunk % 4, slice(chunk // 4 * 128, chunk // 4 * 128 + 128)
-        total = jnp.zeros((1, 128), F32)
         for m in range(2):
             v = b.p2[m * 128 : m * 128 + 128, cols]
             up = b.d_packed[m * 4 + head, :, place].astype(F32)
@@ -963,56 +973,133 @@
             dy = up * b.cosine[...] + half_turn(up * b.sine[...])
             t = dy * b.qk[:, cols]
             dv = r * (t - v * (r * r * head_mean(t * v, b.ones[...])))
-            total += jnp.sum(dy * (v * r), 0, keepdims=True)
+            b.d_qk[chunk // 4 : chunk // 4 + 1] += jnp.sum(dy * (v * r), 0, keepdims=True)
             if chunk >= 4:
                 dv = jnp.where(lanes() < 64, dv, up)
             b.dp2[m * 128 : m * 128 + 128, cols] = low(dv)
-        b.d_qk[chunk : chunk + 1] = total
     for copy in attn_loads:
         copy.wait()
 
     def back2(cols):
-        b.partial[:, cols] = times_transposed(b.dp2[...], b.proj[cols, :1024])
+        b.partial[:, cols] = times_transposed(b.dp2[...], b.proj[cols, :])
 
     by_columns(1024, back2)
-    swap = moves.sibling(b.partial, b.other2)
-
-    ci_loads = [
-        moves.local(w.at[:, pl.ds(2304, 768)], b.proj.at[:, pl.ds(i * 768, 768)])
-        for i, w in enumerate((b.w0, b.w1))
-    ]
+    swap = moves.sibling(b.partial, b.other)
     staged(
         moves,
         b.normed_t,
         lambda k: b.dp2[:, k * 256 : k * 256 + 256],
         slots(b.su, b.sd),
-        places(b.grad0, 3072, 2) + places(b.grad1, 3072, 2),
+        places(b.qw0_grad, 2) + places(b.qw1_grad, 2),
     )
     swap.wait_recv()
-    norm_back_rows(b.z, b.gains[2:3], (b.partial, b.other2), b.dh2, b.dz, b.d_mix1)
-    ring.forward(0)
-
-    norm_rows(b.h1, b.gains[1:2], b.normed)
+    unpermuted(b, b.partial, b.other, b.dn)
+    moves.flush()
+    ring2.start(0)
+    norm_back_rows(b.z, b.gains.at[1, 0:1], (b.dn,), b.dh2, b.dz, b.d_mix1)
+
+    norm_rows(b.h1, b.gains.at[0, 1:2], b.normed)
     transpose_into(b.normed, b.normed_t)
     transpose_into(b.dz, b.turned)
     moves.done(swap)
-    moves.flush()
-    ffn_loop(
-        b,
-        [w.at[:, pl.ds(0, 2304)] for w in (b.w0, b.w1, b.w2)],
-        [w.at[:, pl.ds(0, 2304)] for w in (b.grad0, b.grad1, b.grad2)],
-        b.normed, b.normed_t, b.dz, b.turned, b.partial,
-    )
-    swap = moves.sibling(b.partial, b.other0)
     ring.finish(0)
     ring.start(1)
+    ffn_loop(
+        b, (b.gate0, b.up0, b.down0), (b.gate_grad, b.up_grad, b.down_grad),
+        b.normed, b.normed_t, b.dz, b.turned, b.partial,
+    )
+    swap = moves.sibling(b.partial, b.other0)
+    ring.forward(1)
+    ring2.forward(0)
+    ring.finish(1)
+    ring.start(2)
+    ring2.finish(0)
+    ring2.start(1)
     swap.wait_recv()
-    norm_back_rows(b.h1, b.gains[1:2], (b.partial, b.other0), b.dz, b.dh1, b.d_ffn0)
-
-    def rounded0(rows):
+    norm_back_rows(b.h1, b.gains.at[0, 1:2], (b.partial, b.other0), b.dz, b.dh1, b.d_ffn0)
+    ring.forward(2)
+    ring2.forward(1)
+    ring.finish(2)
+    ring2.finish(1)
+    ring2.start(2)
+    ring2.forward(2)
+    ring2.finish(2)
+    ring.settle()
+    ring2.settle()
+    moves.settle()
+
+
+def own_columns(ref, k):
+    return ref[:, pl.ds(pl.multiple_of(lax.axis_index(S) * 512 + k * 256, 256), 256)]
+
+
+def ring_scratch(first, widths):
+    return {first + str(i): s for i, s in enumerate(scatter_scratch(widths))}
+
+
+def backward(qk, cosine, sine, ones, perm, w, mid):
+    partial_gain = ((8, 1024), F32, VM)
+    wide, thin = ((1024, 2304), BF, ANY), ((1024, 512), BF, ANY)
+    rings = ring_scratch(chr(97), (2304,) * 3), ring_scratch(chr(98), (512,) * 3)
+
+    def body(b):
+        b.ring, b.ring2 = [[getattr(b, name) for name in ring] for ring in rings]
+        backward_kernel(b)
+
+    def sums(width):
+        return ((16, width), F32, VM)
+
+    return launch(
+        body,
+        "backward",
+        3,
+        dict(
+            gains=(w.gains_out, VM), qk=(qk, VM), cosine=(cosine, VM), sine=(sine, VM), ones=(ones, VM),
+            dh2=(mid.dh2, VM), att=(w.att_out, VM), z=(w.z_out, VM), h1=(w.h1_out, VM), perm_in=(perm, ANY),
+            gate0=(flat(w.gate0_out), ANY), up0=(flat(w.up0_out), ANY), down0=(flat(w.down0_out), ANY),
+            qw0=(flat(w.qw0_out), ANY), qw1=(flat(w.qw1_out), ANY), mo1_in=(flat(w.mo1_out), ANY),
+            packed_in=(w.packed_out, ANY), p2_in=(w.p2_out, ANY),
+            rg=(mid.gg.reshape(ring_shape(2304)), ANY), ru=(mid.gu.reshape(ring_shape(2304)), ANY),
+            rd=(mid.gd.reshape(ring_shape(2304)), ANY),
+        ),
+        dict(
+            gate_grad=wide, up_grad=wide, down_grad=wide, qw0_grad=thin, qw1_grad=thin, mo1_grad=thin,
+            d_qk=((8, 128), F32, VM), d_mix1=partial_gain, d_ffn0=partial_gain, dh1=((256, 1024), F32, VM),
+            sum_g=sums(2304), sum_u=sums(2304), sum_d=sums(2304), sum_q0=sums(512), sum_q1=sums(512), sum_mo=sums(512),
+        ),
+        dict(
+            mo=bf(1024, 1024), proj=bf(1024, 1024), perm=bf(1024, 1024),
+            packed=bf(8, 128, 256), p2=vm(256, 1024), do=bf(256, 1024),
+            out_att=bf(8, 128, 128), d_att=bf(8, 128, 128), turned=bf(1024, 256), dkv=vm(1024, 128), out=bf(8, 128, 256),
+            d_packed=bf(8, 128, 256), normed=bf(256, 1024), normed_t=bf(1024, 256), dp2=bf(256, 1024),
+            high=bf(256, 1024), rest=bf(256, 1024), dn=vm(256, 1024),
+            partial=vm(256, 1024), other=vm(256, 1024), other0=vm(256, 1024), dz=bf(256, 1024),
+            local=dma(32), send=dma(24), recv=dma(24), ssend=dma(2, 54), srecv=dma(2, 54), sload=dma(2, 27),
+            **ffn_scratch(), **rings[0], **rings[1],
+        ),
+    )
+
+
+def last_kernel(b):
+    core, seq = lax.axis_index(S), lax.axis_index(SQ)
+    here = chip()
+    around = [device_at(moved(here, axis, by)) for axis in range(3) for by in (1, 2, 3)]
+    greet(around + [sibling_device(), {SQ: lax.rem(seq + 1, 8)}, {SQ: lax.rem(seq + 7, 8)}])
+    moves = Moves(b.local, b.send, b.recv)
+    ring = Scatter((b.rg, b.ru, b.rd), b.ring, (b.sum_g, b.sum_u, b.sum_d), b.ssend.at[0], b.srecv.at[0], b.sload.at[0])
+    ring2 = Scatter(
+        (b.ci0_grad, b.ci1_grad, b.mt_grad), b.ring2, (b.sum_c0, b.sum_c1, b.sum_mt), b.ssend.at[1], b.srecv.at[1], b.sload.at[1]
+    )
+    ring.start(0)
+    mo0_load = moves.local(b.mo0_in, b.mo)
+    p1_load = moves.local(b.p1_in, b.p1)
+    perm_load = moves.local(b.perm_in, b.perm)
+    ci_loads = [moves.local(w, b.ci.at[:, pl.ds(i * 768, 768)]) for i, w in enumerate((b.ci0, b.ci1))]
+
+    def rounded(rows):
         b.do[rows] = low(b.dh1[rows])
 
-    by_rows(256, rounded0)
+    by_rows(256, rounded)
     mo0_load.wait()
     p1_load.wait()
 
@@ -1032,10 +1119,14 @@
     lax.fori_loop(0, 4, mixed, 0)
     rim = moves.remote(b.dconv.at[:, pl.ds(0, 8)], b.rim, {SQ: lax.rem(seq + 7, 8)})
     transpose_into(b.m1, b.turned)
-    staged(moves, b.turned, own_do, slots(b.sg), places(b.grad2, 2304, 2))
-    norm_rows(b.x, b.gains[0:1], b.normed)
-    transpose_into(b.normed, b.normed_t)
-    ring.forward(1)
+    for k in range(2):
+        cols = slice(k * 256, k * 256 + 256)
+        grad = low(matmul(b.turned[...], own_columns(b.do, k)))
+        b.mt_grad[..., cols] = grad.reshape(ring_shape(256))
+    norm_rows(b.x, b.gains.at[0, 0:1], b.normed)
+    perm_load.wait()
+    permuted(b.normed, b.perm, b.high)
+    transpose_into(b.high, b.normed_t)
     rim.wait_recv()
     b.dconv[:, 128:] = jnp.where(seq < 7, b.rim[...], 0.0)
     b.d_taps[...] = jnp.zeros_like(b.d_taps)
@@ -1055,72 +1146,151 @@
         return carry
 
     lax.fori_loop(0, 4, conv_back, 0)
+    for x in range(4):
+        tile = low(b.d_taps[:, x * 128 : x * 128 + 128])
+        b.mt_grad[x, :, :, :, :, 512:] = jnp.broadcast_to(jnp.concatenate([tile, tile], 0), (2, 4, 2, 16, 128))
+    for i, grad in enumerate((b.ci0_grad, b.ci1_grad)):
+        for j in range(3):
+            cols = slice(i * 768 + j * 256, i * 768 + j * 256 + 256)
+            value = low(matmul(b.normed_t[...], b.dp1[:, cols]))
+            grad[..., j * 256 : j * 256 + 256] = value.reshape(ring_shape(256))
+    ring2.start(0)
+    ring.forward(0)
     for copy in ci_loads:
         copy.wait()
-    moves.done(swap)
 
     def back1(cols):
-        b.partial[:, cols] = times_transposed(b.dp1[...], b.proj[cols, :])
+        b.partial[:, cols] = times_transposed(b.dp1[...], b.ci[cols, :])
 
     by_columns(1024, back1)
-    swap = moves.sibling(b.partial, b.other2)
-
-    staged(
-        moves,
-        b.normed_t,
-        lambda k: b.dp1[:, k * 256 : k * 256 + 256],
-        slots(b.su, b.sd, b.wg),
-        places(b.grad0, 2304, 3) + places(b.grad1, 2304, 3),
-    )
+    swap = moves.sibling(b.partial, b.other)
+    swap.wait_recv()
+    unpermuted(b, b.partial, b.other, b.dn)
+    norm_back_rows(b.x, b.gains.at[0, 0:1], (b.dn,), b.dh1, b.dx, b.d_mix0)
+
+    first = core == 0
+    small = Small(b.sums, b.qk_other, b.arrivals, b.small_send, b.small_recv)
+    b.sums[0] = jnp.zeros((8, 1024), F32)
+    b.sums[0, 0:1] = jnp.sum(jnp.where(first, b.d_mix0[...], b.d_mix1[...]), 0, keepdims=True)
+    b.sums[0, 1:2] = jnp.sum(jnp.where(first, b.d_ffn0[...], b.d_ffn1[...]), 0, keepdims=True)
+    small.sibling(b.d_qk).start()
+    small.sibling(b.d_qk).wait_recv()
+    b.sums[0, 2:4, :128] = b.d_qk[0:2] + b.qk_other[0:2]
+    small.start(0)
+    ring.finish(0)
+    ring.start(1)
+    ring2.forward(0)
+    small.finish(0)
+    small.start(1)
+    ring.forward(1)
+    ring2.finish(0)
+    ring2.start(1)
+    small.finish(1)
+    small.start(2)
     ring.finish(1)
     ring.start(2)
-    swap.wait_recv()
-    norm_back_rows(b.x, b.gains[0:1], (b.partial, b.other2), b.dh1, b.dx, b.d_mix0)
+    ring2.forward(1)
+    small.finish(2)
+    b.small[...] = b.sums[3]
     ring.forward(2)
+    ring2.finish(1)
+    ring2.start(2)
     ring.finish(2)
+    ring2.forward(2)
+    ring2.finish(2)
+
+    mine = (pl.ds(pl.multiple_of(core * 8, 8), 8), pl.ds(pl.multiple_of(8 - core * 8, 8), 8))
+    column = 0
+    for ref in (b.sum_c0, b.sum_c1, b.sum_q0, b.sum_q1):
+        width = ref.shape[1]
+        home = b.mix_grad.at[core, :, pl.ds(column, width)]
+        moves.keep(ref.at[mine[0]], home)
+        moves.sibling(ref.at[mine[1]], home)
+        column += width
+    pairs = (
+        (b.gate_grad, 2304, (b.sum_g, b.sum_g1)),
+        (b.up_grad, 2304, (b.sum_u, b.sum_u1)),
+        (b.down_grad, 2304, (b.sum_d, b.sum_d1)),
+        (b.mo_grad, 512, (b.sum_mt, b.sum_mo1)),
+    )
+
+    def trade(k, block):
+        out, n, sources = pairs[k]
+        home = out.at[:, pl.ds(block * n, n)]
+        keep = pltpu.make_async_copy(sources[block].at[:, pl.ds(0, n)], home, b.trade.at[k])
+        give = pltpu.make_async_remote_copy(
+            src_ref=sources[1 - block].at[:, pl.ds(0, n)],
+            dst_ref=home,
+            send_sem=b.trade.at[4 + k],
+            recv_sem=b.trade.at[8 + k],
+            device_id=sibling_device(),
+            device_id_type=MESH,
+        )
+        return keep, give
+
+    for block in range(2):
+
+        @pl.when(core == block)
+        def _():
+            for k in range(4):
+                for copy in trade(k, block):
+                    copy.start()
+
+    for k in range(4):
+        keep, give = trade(k, 0)
+        keep.wait()
+        give.wait()
     ring.settle()
+    ring2.settle()
+    small.settle()
+    small.sibling(b.d_qk).wait_send()
+    for copy in moves.sent[-4:]:
+        copy.wait_recv()
     moves.settle()
 
 
-def backward(x, gains, qk, cosine, sine, ones, taps, wide, saved, mid):
-    full = (4, 2, 4, 2, 16, 2304)
-    partial_gain = ((8, 1024), F32, VM)
-    widths = (2304,) * 3
-    bufs = scatter_scratch(widths)
-    ring = {chr(97 + i // 9) + str(i % 9): s for i, s in enumerate(bufs)}
+def last(x, perm, w, mid, back):
+    rings = ring_scratch(chr(97), (2304,) * 3), ring_scratch(chr(98), (768, 768, 640))
 
     def body(b):
-        b.ring = [getattr(b, name) for name in ring]
-        backward_kernel(b)
+        b.ring, b.ring2 = [[getattr(b, name) for name in ring] for ring in rings]
+        last_kernel(b)
+
+    def out(*shape, where=ANY):
+        return (shape, F32, where)
+
+    def sums(width):
+        return vm(16, width)
 
     return launch(
         body,
-        "backward",
-        3,
+        "last",
+        4,
         dict(
-            x=(x, VM), gains=(gains, VM), qk=(qk, VM), cosine=(cosine, VM), sine=(sine, VM),
-            ones=(ones, VM), taps=(taps, VM), dh2=(mid.dh2, VM), att=(saved.att_out, VM), z=(saved.z_out, VM),
-            h1=(saved.h1_out, VM), m1=(saved.m1_out, VM), pad=(saved.pad_out, VM),
-            w0=(wide[0], ANY), w1=(wide[1], ANY), w2=(wide[2], ANY),
-            mo0_in=(saved.mo0_out, ANY), mo1_in=(saved.mo1_out, ANY), packed_in=(saved.packed_out, ANY),
-            p2_in=(saved.p2_out, ANY), p1_in=(saved.p1_out, ANY),
-            rg=(mid.gg.reshape(full), ANY), ru=(mid.gu.reshape(full), ANY), rd=(mid.gd.reshape(full), ANY),
+            x=(x, VM), gains=(w.gains_out, VM), taps=(w.taps_out, VM), dh1=(back.dh1, VM), m1=(w.m1_out, VM),
+            pad=(w.pad_out, VM), d_qk=(back.d_qk, VM), d_mix1=(back.d_mix1, VM), d_ffn0=(back.d_ffn0, VM),
+            d_ffn1=(mid.d_ffn, VM), mo0_in=(flat(w.mo0_out), ANY), p1_in=(w.p1_out, ANY), perm_in=(perm, ANY),
+            ci0=(flat(w.ci0_out), ANY), ci1=(flat(w.ci1_out), ANY),
+            rg=(back.gate_grad.reshape(ring_shape(2304)), ANY), ru=(back.up_grad.reshape(ring_shape(2304)), ANY),
+            rd=(back.down_grad.reshape(ring_shape(2304)), ANY),
+            sum_g1=(back.sum_g, VM), sum_u1=(back.sum_u, VM), sum_d1=(back.sum_d, VM),
+            sum_q0=(back.sum_q0, VM), sum_q1=(back.sum_q1, VM), sum_mo1=(back.sum_mo, VM),
         ),
         dict(
-            grad0=((1024, 3584), BF, ANY), grad1=((1024, 3584), BF, ANY), grad2=((1024, 3328), BF, ANY),
-            d_qk=((8, 128), F32, VM), d_mix1=partial_gain, d_ffn0=partial_gain, d_mix0=partial_gain,
-            d_taps=((8, 512), F32, VM), dx=((256, 1024), BF, VM),
-            sum_g=((16, 2304), F32, VM), sum_u=((16, 2304), F32, VM), sum_d=((16, 2304), F32, VM),
+            dx=((256, 1024), BF, VM), small=out(8, 1024, where=VM), mix_grad=out(2, 8, 2560),
+            gate_grad=out(16, 4608), up_grad=out(16, 4608), down_grad=out(16, 4608), mo_grad=out(16, 1024),
+            sum_mt=out(16, 640, where=VM),
         ),
         dict(
-            mo=bf(1024, 1024), proj=bf(1024, 1536),
-            packed=bf(8, 128, 256), p2=vm(256, 1024), p1=vm(256, 1536), do=bf(256, 1024),
-            out_att=bf(8, 128, 128), d_att=bf(8, 128, 128), turned=bf(1024, 256), dkv=vm(1024, 128), out=bf(8, 128, 256),
-            d_packed=bf(8, 128, 256), normed=bf(256, 1024), normed_t=bf(1024, 256), dp2=bf(256, 1024),
-            partial=vm(256, 1024), other2=vm(256, 1024), other0=vm(256, 1024),
-            dz=bf(256, 1024), dh1=vm(256, 1024), dp1=bf(256, 1536), dconv=vm(2, 136, 512), rim=vm(2, 8, 512),
-            local=dma(32), send=dma(24), recv=dma(24), ssend=dma(54), srecv=dma(54), sload=dma(27),
-            **ffn_scratch(), **ring,
+            mo=bf(1024, 1024), ci=bf(1024, 1536), perm=bf(1024, 1024), p1=vm(256, 1536), do=bf(256, 1024),
+            turned=bf(1024, 256), normed=bf(256, 1024), normed_t=bf(1024, 256), high=bf(256, 1024),
+            rest=bf(256, 1024), dn=vm(256, 1024), partial=vm(256, 1024), other=vm(256, 1024),
+            dp1=bf(256, 1536), dconv=vm(2, 136, 512), rim=vm(2, 8, 512), d_taps=vm(8, 512), d_mix0=vm(8, 1024),
+            ci0_grad=bf(*ring_shape(768)), ci1_grad=bf(*ring_shape(768)), mt_grad=bf(*ring_shape(640)),
+            sum_g=sums(2304), sum_u=sums(2304), sum_d=sums(2304), sum_c0=sums(768), sum_c1=sums(768),
+            sums=vm(4, 8, 1024), qk_other=vm(8, 128), arrivals=vm(9, 8, 1024), small_send=dma(10), small_recv=dma(10),
+            local=dma(16), send=dma(12), recv=dma(12), trade=dma(12),
+            ssend=dma(2, 54), srecv=dma(2, 54), sload=dma(2, 27), **rings[0], **rings[1],
         ),
     )
 
@@ -1141,57 +1311,18 @@
     return lax.dot_general(left, right, (((0,), (0,)), ((), ())), preferred_element_type=F32)
 
 
-def swapped(value):
-    return lax.ppermute(value, S, [(0, 1), (1, 0)])
-
-
-def core_half(value, which, axis=1):
-    size = value.shape[axis] // 2
-    return lax.dynamic_slice_in_dim(value, which * size, size, axis)
-
-
-def row_homes(turn):
-    pairs = []
-    for s in range(2):
-        for i in range(64):
-            core = (i % 2) ^ turn
-            pairs.append((s * 64 + i, core * 64 + s * 32 + i // 2))
-    return pairs
-
-
-def mixer_halves(conv_in, qkv):
-    def half(core):
-        b = conv_in.reshape(8, 3, 2, 512)
-        b = lax.dynamic_index_in_dim(b, core, 2, False).reshape(8, 1536)
-        q = core_half(qkv[:, :1024], core)
-        k = core_half(qkv[:, 1024:1536], core).reshape(8, 4, 64)
-        v = core_half(qkv[:, 1536:], core).reshape(8, 4, 64)
-        return jnp.concatenate([b, q, jnp.concatenate([k, v], 2).reshape(8, 512)], 1)
-
-    odd = lax.axis_index(SQ) % 2
-    got = [
-        lax.ppermute(half(jnp.bitwise_xor(odd, turn)), (S, DP, SQ), row_homes(turn))
-        for turn in range(2)
-    ]
-    first = lax.axis_index(S) == 0
-    return jnp.concatenate([jnp.where(first, got[0], got[1]), jnp.where(first, got[1], got[0])], 0)
-
-
-def mixer_homes(grads):
-    core = lax.axis_index(S)
-    got = []
-    for turn in range(2):
-        parity = jnp.bitwise_xor(core, turn)
-        rows = lax.dynamic_slice_in_dim(grads, parity * 8, 8, 0)
-        got.append(lax.ppermute(rows, (S, DP, SQ), [(b, a) for a, b in row_homes(turn)]))
-    even = lax.axis_index(SQ) % 2 == 0
-    lower = jnp.where(even, got[0], got[1])
-    upper = jnp.where(even, got[1], got[0])
-    both = jnp.stack([lower, upper], 1)
-    conv = both[:, :, :1536].reshape(8, 2, 3, 512).transpose(0, 2, 1, 3).reshape(8, 3072)
-
-    kv = both[:, :, 2048:].reshape(8, 2, 4, 2, 64).transpose(0, 3, 1, 2, 4).reshape(8, 1024)
-    return conv, jnp.concatenate([both[:, :, 1536:2048].reshape(8, 1024), kv], 1)
+def both_halves(conv_in, qkv):
+    b = conv_in.reshape(8, 3, 2, 512).transpose(2, 0, 1, 3).reshape(2, 8, 1536)
+    q = qkv[:, :1024].reshape(8, 2, 512).transpose(1, 0, 2)
+    kv = qkv[:, 1024:].reshape(8, 2, 2, 4, 64).transpose(2, 0, 3, 1, 4).reshape(2, 8, 512)
+    return jnp.concatenate([b, q, kv], 2)
+
+
+def from_halves(grads):
+    conv = grads[:, :, :1536].reshape(2, 8, 3, 512).transpose(1, 2, 0, 3).reshape(8, 3072)
+    q = grads[:, :, 1536:2048].transpose(1, 0, 2).reshape(8, 1024)
+    kv = grads[:, :, 2048:].reshape(2, 8, 4, 2, 64).transpose(1, 3, 0, 2, 4).reshape(8, 1024)
+    return conv, jnp.concatenate([q, kv], 1)
 
 
 def rope_tables():
@@ -1217,75 +1348,42 @@
     w_down,
 ):
     core = lax.axis_index(S)
-    first = core == 0
+    place = lax.axis_index((DP, SQ)) % 16 * 8
     x = inputs.reshape(256, 1024)
     cot = cotangent.reshape(256, 1024)
-    gains = lax.all_gather(jnp.concatenate([mix_gain, ffn_gain], 0), S).astype(F32)
+    gains = jnp.pad(jnp.concatenate([mix_gain, ffn_gain], 0).astype(F32), ((0, 6), (0, 0)))
     qk = qk_gain.astype(F32)
-
-    own = [mix_out[0], w_gate[0], w_up[0], w_down[0].T]
-    keep = jnp.concatenate([core_half(w, core) for w in own], 1)
-    got = swapped(jnp.concatenate([core_half(w, 1 - core) for w in own], 1))
-    block0, block1 = jnp.where(first, keep, got), jnp.where(first, got, keep)
-    cuts = (512, 2816, 5120)
-    mo0, g0, u0, d0 = jnp.split(block0, cuts, 1)
-    mo1, g1, u1, d1 = jnp.split(block1, cuts, 1)
-    mixers = mixer_halves(conv_in, qkv_weight)
-    ci, qw = mixers[:, :1536], mixers[:, 1536:]
-    taps = jnp.pad(conv_kernel, ((0, 13), (0, 120)))
-    early = [
-        jnp.concatenate([g0, ci[:, :768], qw[:, :512]], 1),
-        jnp.concatenate([u0, ci[:, 768:], qw[:, 512:]], 1),
-        jnp.concatenate([d0, mo0, mo1, taps], 1),
-    ]
-    wide = [b.reshape(1024, -1) for b in gathered(early, 0)]
-    taps = wide[2][:, 3328:].reshape(64, 16, 128)[:, :3, :8].transpose(1, 0, 2).reshape(3, 512)
-    taps = jnp.pad(taps.astype(F32), ((0, 5), (0, 0)))
-    gains = jnp.pad(jnp.stack([gains[0, 0], gains[0, 1], gains[1, 0], gains[1, 1]]), ((0, 4), (0, 0)))
     kv_gain = jnp.concatenate([qk[1], jnp.ones((64,), F32)])
     qk_row = jnp.concatenate([jnp.tile(qk[0], 8), jnp.tile(kv_gain, 4)])[None]
     cosine, sine = rope_tables()
     lane = jnp.arange(128)
     ones = ((lane[:, None] // 64) == (lane[None, :] // 64)).astype(F32) / 64.0
-    common = (x, gains, qk_row, cosine, sine, ones, taps, wide)
-    saved = forward(*common, (g1, u1, d1))
-    mid = middle(saved.h2_out, cot, gains, saved)
+    row = jnp.arange(1024)
+    natural = row % 16 // 8 * 512 + row // 16 * 8 + row % 8
+    perm = (row[:, None] == natural[None, :]).astype(BF)
+    taps = lax.dynamic_update_slice(jnp.zeros((16, 128), BF), conv_kernel, (0, place))
+    mix = both_halves(conv_in, qkv_weight).astype(F32)
+    common = (qk_row, cosine, sine, ones, perm)
+    saved = forward(x, gains, *common, taps, mix, (w_gate[0], w_up[0], w_down[0].T, mix_out[0]))
+    mid = middle(cot, saved)
     back = backward(*common, saved, mid)
-
-    taps_grad = jnp.pad(back.d_taps[:3].reshape(3, 64, 8).transpose(1, 0, 2), ((0, 0), (0, 13), (0, 120)))
-    parts = [back.grad0, back.grad1, jnp.concatenate([back.grad2, low(taps_grad.reshape(1024, 128))], 1)]
-    d_mix0, d_ffn0, d_mix1, d_ffn1 = [
-        jnp.sum(g, 0) for g in (back.d_mix0, back.d_ffn0, back.d_mix1, mid.d_ffn)
-    ]
-    d_gains = jnp.stack([jnp.where(first, d_mix0, d_mix1), jnp.where(first, d_ffn0, d_ffn1)])
-    d_q = jnp.sum(back.d_qk[:4].reshape(8, 64), 0)
-    d_qk = jnp.concatenate([d_q, jnp.sum(back.d_qk[4:, :64], 0)])[None]
-    small = jnp.concatenate([d_gains.reshape(16, 128), jnp.pad(d_qk, ((0, 7), (0, 0)))], 0)
-    *sums, small = scattered(parts, 4, small)
-
-    block0 = [sums[2][:, 2304:2816], sums[0][:, :2304], sums[1][:, :2304], sums[2][:, :2304]]
-    block1 = [sums[2][:, 2816:3328]] + [back.sum_g, back.sum_u, back.sum_d]
-    block0, block1 = jnp.concatenate(block0, 1), jnp.concatenate(block1, 1)
-    mine = jnp.where(first, block0, block1)
-    theirs = swapped(jnp.where(first, block1, block0))
-    lower = jnp.split(jnp.where(first, mine, theirs), cuts, 1)
-    upper = jnp.split(jnp.where(first, theirs, mine), cuts, 1)
-    mo_grad, g_grad, u_grad, d_grad = [jnp.concatenate(p, 1) for p in zip(lower, upper)]
-    mixers = jnp.concatenate([sums[0][:, 2304:3072], sums[1][:, 2304:3072], sums[0][:, 3072:], sums[1][:, 3072:]], 1)
-    conv_in_grad, qkv_grad = mixer_homes(mixers)
+    end = last(x, perm, saved, mid, back)
+    conv_in_grad, qkv_grad = from_halves(end.mix_grad)
+    half = lax.dynamic_slice_in_dim(end.dx, core * 512, 512, 1)
+    q_sum, k_sum = end.small[2, :128], end.small[3, :64]
     return (
         mid.result.reshape(2, 1, 128, 512),
-        core_half(back.dx, core).reshape(2, 1, 128, 512),
+        half.reshape(2, 1, 128, 512),
         conv_in_grad,
-        sums[2][:3, 3328:3336],
+        lax.dynamic_slice(end.sum_mt, (0, 512 + place), (3, 8)),
         qkv_grad,
-        small[16].reshape(2, 64),
-        small[:8].reshape(1, 1024),
-        small[8:16].reshape(1, 1024),
-        mo_grad[None],
-        g_grad[None],
-        u_grad[None],
-        d_grad.T[None],
+        jnp.stack([q_sum[:64] + q_sum[64:], k_sum]),
+        end.small[0:1],
+        end.small[1:2],
+        end.mo_grad[None],
+        end.gate_grad[None],
+        end.up_grad[None],
+        end.down_grad.T[None],
     )
 
 

time: 491 us -> 445 us (0.906)
  starting transfers between devices: 14.1 us -> 0 us
  Pallas kernels: 422 us -> 409 us
  other arithmetic: 21.7 us -> 9.46 us
  waiting for transfers between devices: 5.43 us -> 0 us
    pallas_call x2 -> x0, Pallas kernels: 192 us -> none  [the longest x1 101 us: gathered(): pl.pallas_call(gather_kernel, name='gather', out_shape=[jax.ShapeDtypeStr...]
    pallas_call x3 -> x4, Pallas kernels: 230 us -> 409 us  [launch(): pl.pallas_call(kernel, name=name, out_shape=[jax.ShapeDtypeStruct(shape,...]
    ppermute x6 -> x0, starting transfers between devices: 14.1 us -> none  [the longest x2 5.67 us: mixer_halves(): lax.ppermute(half(jnp.bitwise_xor(odd, turn)), (S, DP, SQ), row_homes(turn))]
    slice x17 -> x4, local copies, waits for them, and re-layouts: 13.8 us -> 3.85 us  [the longest x1 1.44 us: shards(): end.small[1:2]]
    concatenate x12 -> x1, other arithmetic: 10.2 us -> 0.64 us  [from_halves(): return (conv, jnp.concatenate([q, kv], 1))]
    unnamed x17 -> x9, local copies, waits for them, and re-layouts: 0.8 us -> 7.27 us
    ppermute x6 -> x0, waiting for transfers between devices: 5.43 us -> none  [the longest x2 5.42 us: mixer_homes(): lax.ppermute(rows, (S, DP, SQ), [(b, a) for a, b in row_homes(turn)])]
  transfers between devices with their start and end apart: 6 -> 0, of which waited for: 2 -> 0; matrix products, arithmetic and copies ran while one was open for 2% -> 0% of each run, Pallas kernels for 0% -> 0%
where the time goes in v2:
time: 445 us; the launch traced here: 438 us
  Pallas kernels  409 us (92%)
  local copies, waits for them, and re-layouts  17.6 us (4%)
  other arithmetic  9.46 us (2%)
    pallas_call x4, Pallas kernels, launch(): pl.pallas_call(kernel, name=name, out_shape=[jax.ShapeDtypeStruct(shape,...  409 us

profile of v2, /device:TPU:1, one launch (start us, length us, event | category | flops | bytes accessed | tf_op | source)
XLA Modules:
  0.0 437.6 jit_solution(92238351189642674)
XLA Ops:
  0.7 0.7 convert_element_type.31
  2.1 1.5 dynamic_update_slice.3.refs_7_
  3.6 1.3 fusion.5.refs_1_
  5.0 0.7 fusion.29
  5.9 0.8 copy.30
  6.7 0.7 compare_select_fusion.refs_5_.refs_4_
  7.4 0.7 maximum_convert_fusion.refs_8_
  8.4 0.8 pad_maximum_fusion
  9.3 2.3 fusion.refs_6_.refs_9_.refs_12_
  11.5 173.6 %forward.1 = (bf16[4,2,4,2,16,2304]{5,4,3,2,1,0:T(8,128)(2,1)}, bf16[4,2,4,2,16,2304]{5,4,3,2,1,0:T(8,128)(2,1)}, bf16[4,2,4,2,16,2304]{5,4,3,2,1,0:T(8,128)(2,1...) custom-call(bf16[256,1024]{1,0:T(8,128)(2,1)} %bitcast.74, ...), custom_call_target="tpu_custom_call" | custom-call | tf_op jit(solution)/shard_map/forward/pallas_call | solution.py:293
  185.2 26.8 %middle.1 = (bf16[1024,2304]{1,0:T(8,128)(2,1)}, bf16[1024,2304]{1,0:T(8,128)(2,1)}, bf16[1024,2304]{1,0:T(8,128)(2,1)}, f32[256,1024]{1,0:T(8,128)}, f32[8,1024]{1,0:T(8,128)}, /*index=5*/bf16[256,512]{1,0:T(8,128)(2,1)}) custom-call(f32[256,1024]{1,0:T(8,128)} %get-tuple-element.62.refs_0_, bf16[256,1024]{1,0:T(8,128)(2,1)} %bitcast.81, ...), custom_call_target="tpu_custom_call" | custom-call | tf_op jit(solution)/shard_map/middle/pallas_call | solution.py:293
  212.0 113.1 %backward.1 = (bf16[1024,2304]{1,0:T(8,128)(2,1)}, bf16[1024,2304]{1,0:T(8,128)(2,1)}, bf16[1024,2304]{1,0:T(8,128)(2,1)}, bf16[1024,512]{1,0:T(8,128)(2,1)}, bf...) custom-call(f32[2,8,1024]{2,1,0:T(8,128)} %get-tuple-element.63.refs, ...), custom_call_target="tpu_custom_call" | custom-call | tf_op jit(solution)/shard_map/backward/pallas_call | solution.py:293
  325.1 95.7 %last.1 = (bf16[256,1024]{1,0:T(8,128)(2,1)}, f32[8,1024]{1,0:T(8,128)}, f32[2,8,2560]{2,1,0:T(8,128)}, f32[16,4608]{1,0:T(8,128)}, f32[16,4608]{1,0:T(8,128)}, ...) custom-call(bf16[256,1024]{1,0:T(8,128)(2,1)} %bitcast.75, ...), custom_call_target="tpu_custom_call" | custom-call | tf_op jit(solution)/shard_map/last/pallas_call | solution.py:293
  420.8 1.7 constant_dynamic-slice_fusion.1
  422.5 0.9 slice_add_fusion
  423.4 1.4 fusion.28
  425.4 1.3 constant_dynamic-slice_fusion
  426.7 0.8 fusion.27
  427.5 0.9 slice.45
  429.9 0.7 copy.43
  430.6 1.5 copy.44
  432.1 1.7 copy.45
  433.8 1.7 copy.46
  435.5 1.7 copy.47
  (25 shorter events, 3.4 us)
Async XLA Ops:
  3.6 7.9 %copy-start.1 = (bf16[16,128]{1,0:T(8,128)(2,1)}, bf16[16,128]{1,0:T(8,128)(2,1)S(1)}, u32[]{:S(2)}) copy-start(bf16[16,128]{1,0:T(8,128)(2,1)S(1)} %dynamic_update_slice.3.refs_7_) | copy-start | bytes 12292
  325.1 104.8 %copy-start = (bf16[256,512]{1,0:T(8,128)(2,1)S(1)}, bf16[256,512]{1,0:T(8,128)(2,1)}, u32[]{:S(2)}) copy-start(bf16[256,512]{1,0:T(8,128)(2,1)} %get-tuple-element.67) | copy-start | bytes 786436
